TPU v7x, 256 devices: a whole 4x4x8 slice. The times are simulated.
256 devices in a mesh: lat: 16 (over y_hi, z), lon: 16 (over x, y_lo, core).
Axes of the slice: x: 4, y: 4 (y_hi: 2, y_lo: 2; y = y_hi * 2 + y_lo), z: 8, core: 2. Of those that a mesh axis runs over, the one named last changes fastest.
Arguments:
- tokens: bfloat16 [192, 768, 4, 512], P('lat', 'lon'), may hold values from -100 to 240
- w_qkv: bfloat16 [2, 512, 1536], replicated, may hold values from -16 to 16
- w_out: bfloat16 [2, 512, 512], replicated, may hold values from -0.25 to 0.25
- modulation: float32 [2, 3, 512], replicated, may hold values from -2.5 to 2.5
- w_merge: bfloat16 [2048, 1024], replicated, may hold values from -0.125 to 0.125
Outputs:
- merged_tokens: bfloat16 [96, 384, 4, 1024], P('lat', 'lon')
All inputs are finite; a program needn't handle non-finite values.
Results may differ from a plain program's by a relative error of at most 0.012.
Values may be sent and summed in bfloat16 or wider, within the bound.
No kernel may reach another device: no remote copies, remote signals or barrier semaphores. Data moves between devices by JAX's collectives and lax.ppermute only.
A program may use at most 128 MiB of HBM per device.

v0:
```python
import functools
import math

import jax
import jax.numpy as jnp
from jax import lax
from jax.experimental import pallas as pl
from jax.experimental.pallas import tpu as pltpu
from jax.sharding import PartitionSpec as P

HEADS = 16
WIN = 12
HALF = 6
QUAD = 72
SPAN = 4 * QUAD
WIDTH = 512
HEAD = WIDTH // HEADS
GROUP = 8
MAIN = 256
REST = SPAN - MAIN
SUB = 18
FAR = -1e30
SCALE = math.log2(math.e) / math.sqrt(HEAD)
NT = (((1,), (1,)), ((), ()))


def dot(a, b):
    return jnp.dot(a, b, preferred_element_type=jnp.float32)


def dot_nt(a, b):
    return lax.dot_general(a, b, NT, preferred_element_type=jnp.float32)


def normalized(values, eps):
    centered = values - jnp.mean(values, axis=-1, keepdims=True)
    return centered * lax.rsqrt(jnp.mean(centered * centered, axis=-1, keepdims=True) + eps)


def softened(scores, apart, straddles):
    half = SPAN // 2
    top, bottom = scores[:half], scores[half:]
    if apart is None:
        most = jnp.maximum(jnp.max(top, axis=0, keepdims=True), jnp.max(bottom, axis=0, keepdims=True))
        return jnp.exp2(scores - most).astype(jnp.bfloat16)
    if straddles:
        lane = lax.broadcasted_iota(jnp.int32, (1, MAIN), 1)
        from_top = jnp.where(lane < half, 0.0, apart)
        from_bottom = jnp.where(lane < half, apart, 0.0)
    else:
        from_top = jnp.full((1, MAIN), apart, jnp.float32)
        from_bottom = jnp.zeros((1, MAIN), jnp.float32)
    most = jnp.maximum(
        jnp.max(top, axis=0, keepdims=True) + from_top, jnp.max(bottom, axis=0, keepdims=True) + from_bottom
    )
    return jnp.concatenate(
        [
            jnp.exp2(top - (most - from_top)).astype(jnp.bfloat16),
            jnp.exp2(bottom - (most - from_bottom)).astype(jnp.bfloat16),
        ],
        axis=0,
    )


def attend_window(grid, wqk_ref, wvt_ref, wout_ref, mod_ref, vt_ref, att_ref, apart):
    hidden = (normalized(grid, 1e-06) * (1.0 + mod_ref[0:1]) + mod_ref[1:2]).astype(jnp.bfloat16)
    query = (dot(hidden, wqk_ref[:, :WIDTH]) * SCALE).astype(jnp.bfloat16)
    keys = dot(hidden, wqk_ref[:, WIDTH:]).astype(jnp.bfloat16)
    vt_ref[...] = dot_nt(wvt_ref[...], hidden).astype(jnp.bfloat16)
    ones = jnp.ones((16, SPAN), jnp.bfloat16)
    wide = GROUP * HEAD
    lane_head = lax.broadcasted_iota(jnp.int32, (1, wide), 1) // HEAD
    same = (
        lax.broadcasted_iota(jnp.int32, (wide, wide), 0) // HEAD
        == lax.broadcasted_iota(jnp.int32, (wide, wide), 1) // HEAD
    )
    fold = (
        lax.broadcasted_iota(jnp.int32, (REST, wide), 0) == lax.broadcasted_iota(jnp.int32, (REST, wide), 1) % HEAD
    ).astype(jnp.bfloat16)
    eye = (
        lax.broadcasted_iota(jnp.int32, (MAIN, MAIN), 0) == lax.broadcasted_iota(jnp.int32, (MAIN, MAIN), 1)
    ).astype(jnp.bfloat16)
    rest = []
    for group in range(HEADS // GROUP):
        cols = slice(group * wide, (group + 1) * wide)
        qg, kg = query[:, cols], keys[:, cols]
        for item in range(GROUP):
            head = group * GROUP + item
            own = (lane_head == item).astype(jnp.bfloat16)
            weights = softened(dot_nt(kg, qg[:MAIN] * own), apart, True)
            mixed = dot(jnp.concatenate([vt_ref[head * HEAD : (head + 1) * HEAD], ones], axis=0), weights)
            att_ref[head * HEAD : (head + 1) * HEAD] = (mixed[:HEAD] * (1.0 / mixed[HEAD : HEAD + 1])).astype(
                jnp.bfloat16
            )
        spread = jnp.concatenate([qg[MAIN:]] * GROUP, axis=0) * same.astype(jnp.bfloat16)
        weights = softened(dot_nt(kg, spread), apart, False)
        mixed = dot(jnp.concatenate([vt_ref[cols], ones], axis=0), weights)
        mixed = jnp.where(same, mixed[:wide] * (1.0 / mixed[wide : wide + 1]), 0.0).astype(jnp.bfloat16)
        rest.append(dot_nt(fold, mixed).astype(jnp.bfloat16))
    main = dot_nt(eye, att_ref[...]).astype(jnp.bfloat16)
    attended = jnp.concatenate([main, jnp.concatenate(rest, axis=1)], axis=0)
    return grid + (1.0 + mod_ref[2:3]) * dot(attended, wout_ref[...])


def first_kernel(
    level, tokens_ref, wqk_ref, wvt_ref, wout_ref, mod_ref, up_ref, stay_top_ref, down_ref, stay_low_ref, west_ref,
    grid_ref, vt_ref, att_ref,
):
    window = pl.program_id(0)
    for quad in range(4):
        for sub in range(4):
            for place in range(9):
                i = quad // 2 * HALF + place // 3 * 2 + sub % 2
                j = quad % 2 * HALF + place % 3 * 2 + sub // 2
                row = quad * QUAD + sub * SUB + place * 2
                grid_ref[row : row + 2] = tokens_ref[i, j, level : level + 2].astype(jnp.float32)
    out = attend_window(grid_ref[...], wqk_ref, wvt_ref, wout_ref, mod_ref, vt_ref, att_ref, None)
    for side in range(2):
        block = 2 * window + side
        top = out[side * QUAD : (side + 1) * QUAD].astype(jnp.bfloat16)
        low = out[(2 + side) * QUAD : (3 + side) * QUAD].astype(jnp.bfloat16)
        stays = jnp.logical_and(block >= 1, block <= 4)

        @pl.when(stays)
        def _():
            stay_top_ref[block - 1] = top
            down_ref[block - 1] = low

        @pl.when(jnp.logical_not(stays))
        def _():
            up_ref[(block + 3) % 8] = top

        @pl.when(block >= 5)
        def _():
            stay_low_ref[block - 5] = low

        @pl.when(block == 0)
        def _():
            west_ref[0] = low


def second_kernel(
    apart_ref, stay_top_ref, above_ref, stay_low_ref, below_ref, east_low_ref, east_top_ref,
    wqk_ref, wvt_ref, wout_ref, mod_ref, merge_ref,
    back_up_ref, own_top_ref, own_low_ref, back_down_ref, back_east_ref,
    grid_ref, vt_ref, att_ref, joined_ref,
):
    window = pl.program_id(0)

    def put(quad, piece):
        grid_ref[quad * QUAD : (quad + 1) * QUAD] = piece.astype(jnp.float32)

    @pl.when(window < 2)
    def _():
        for side in range(2):
            put(side, above_ref[2 * window + side])
            put(2 + side, stay_top_ref[2 * window + side])

    @pl.when(window >= 2)
    def _():
        put(0, stay_low_ref[2 * window - 4])
        put(2, below_ref[2 * window - 4])

    @pl.when(window == 2)
    def _():
        put(1, stay_low_ref[1])
        put(3, below_ref[1])

    @pl.when(window == 3)
    def _():
        put(1, east_low_ref[0])
        put(3, east_top_ref[0])

    apart = jnp.where(window < 2, apart_ref[0], apart_ref[1])
    out = attend_window(grid_ref[...], wqk_ref, wvt_ref, wout_ref, mod_ref, vt_ref, att_ref, apart)
    grid_ref[...] = out.astype(jnp.bfloat16).astype(jnp.float32)
    for quad in range(4):
        for sub in range(4):
            start = quad * QUAD + sub * SUB
            joined_ref[window, quad * SUB : (quad + 1) * SUB, sub * WIDTH : (sub + 1) * WIDTH] = grid_ref[
                start : start + SUB
            ]

    @pl.when(window == 3)
    def _():
        flat = jnp.concatenate([normalized(joined_ref[w], 1e-05).astype(jnp.bfloat16) for w in range(4)], axis=0)
        merged = dot(flat, merge_ref[...])

        def piece(w, quad):
            return merged[w * QUAD + quad * SUB : w * QUAD + (quad + 1) * SUB].astype(jnp.bfloat16)

        for w in range(2):
            for side in range(2):
                back_up_ref[2 * w + side] = piece(w, side)
                own_top_ref[2 * w + side] = piece(w, 2 + side)
        own_low_ref[0], own_low_ref[1], own_low_ref[2] = piece(2, 0), piece(2, 1), piece(3, 0)
        back_down_ref[0], back_down_ref[1] = piece(2, 2), piece(2, 3)
        back_down_ref[2], back_down_ref[3] = piece(3, 2), piece(3, 3)
        back_east_ref[0] = piece(3, 1)


def last_kernel(*refs):
    out_ref = refs[-1]
    for pair in range(2):
        own_top, own_low, from_below, from_above, corner, from_west = refs[6 * pair : 6 * pair + 6]
        sources = {(0, 0): (corner, 0), (1, 0): (from_west, 0)}
        for c in range(4):
            sources[0, c + 1], sources[1, c + 1] = (own_top, c), (from_below, c)
        for c in range(3):
            sources[0, c + 5], sources[1, c + 5] = (from_above, c), (own_low, c)
        for (half, block), (ref, index) in sources.items():
            for place in range(9):
                i, j = half * 3 + place // 3, block * 3 + place % 3
                out_ref[i, j, 2 * pair : 2 * pair + 2] = ref[index, 2 * place : 2 * place + 2]


def whole(*shape):
    return pl.BlockSpec(shape, lambda w: (0,) * len(shape))


def struct(*shape):
    return jax.ShapeDtypeStruct(shape, jnp.bfloat16)


LIMIT = 48 * 1024 * 1024
LAYER_SCRATCH = [
    pltpu.VMEM((SPAN, WIDTH), jnp.float32),
    pltpu.VMEM((WIDTH, SPAN), jnp.bfloat16),
    pltpu.VMEM((WIDTH, MAIN), jnp.bfloat16),
]
LAYER_SPECS = [whole(WIDTH, 2 * WIDTH), whole(WIDTH, WIDTH), whole(WIDTH, WIDTH), whole(3, WIDTH)]
LAYER_FLOPS = 2 * 4 * SPAN * (4 * WIDTH * WIDTH + 2 * 8 * SPAN * WIDTH)


def first_layer(level, tokens, layer):
    counts = (4, 4, 4, 3, 1)
    return pl.pallas_call(
        functools.partial(first_kernel, level),
        grid=(4,),
        in_specs=[pl.BlockSpec((WIN, WIN, 4, WIDTH), lambda w: (0, w, 0, 0))] + LAYER_SPECS,
        out_specs=[whole(n, QUAD, WIDTH) for n in counts],
        out_shape=[struct(n, QUAD, WIDTH) for n in counts],
        scratch_shapes=LAYER_SCRATCH,
        compiler_params=pltpu.CompilerParams(vmem_limit_bytes=LIMIT),
        cost_estimate=pl.CostEstimate(flops=LAYER_FLOPS, bytes_accessed=5 << 20, transcendentals=16 * 4 * SPAN * SPAN),
        name=f"layer0_level{level}",
    )(tokens, *layer)


def second_layer(apart, pieces, layer, w_merge):
    outs = (4, 4, 3, 4, 1)
    return pl.pallas_call(
        second_kernel,
        grid=(4,),
        in_specs=[pl.BlockSpec(memory_space=pltpu.SMEM)]
        + [whole(p.shape[0], QUAD, WIDTH) for p in pieces]
        + LAYER_SPECS
        + [whole(4 * WIDTH, 2 * WIDTH)],
        out_specs=[whole(n, SUB, 2 * WIDTH) for n in outs],
        out_shape=[struct(n, SUB, 2 * WIDTH) for n in outs],
        scratch_shapes=LAYER_SCRATCH + [pltpu.VMEM((4, QUAD, 4 * WIDTH), jnp.float32)],
        compiler_params=pltpu.CompilerParams(vmem_limit_bytes=LIMIT),
        cost_estimate=pl.CostEstimate(
            flops=LAYER_FLOPS + 2 * SPAN * 8 * WIDTH * WIDTH, bytes_accessed=8 << 20, transcendentals=16 * 4 * SPAN * SPAN
        ),
        name="layer1_merge",
    )(apart, *pieces, *layer, w_merge)


def moved(value, axis, steps):
    count = lax.axis_size(axis)
    return lax.ppermute(value, axis, [(source, (source + steps) % count) for source in range(count)])


def body(tokens, w_qkv, w_out, modulation, w_merge):
    wqk = w_qkv[:, :, : 2 * WIDTH]
    wvt = jnp.swapaxes(w_qkv[:, :, 2 * WIDTH :], 1, 2)
    layers = [(wqk[i], wvt[i], w_out[i], modulation[i]) for i in range(2)]
    lat, last = lax.axis_index("lat"), lax.axis_size("lat") - 1
    apart = jnp.where(jnp.stack([lat == 0, lat == last]), FAR, 0.0).astype(jnp.float32)
    firsts = [first_layer(level, tokens, layers[0]) for level in (0, 2)]
    seconds = []
    for up, stay_top, down, stay_low, west in firsts:
        below = moved(up, "lat", -1)
        above = moved(down, "lat", 1)
        east_low = moved(west, "lon", -1)
        east_top = moved(below[3:], "lon", -1)
        pieces = (stay_top, above, stay_low, below, east_low, east_top)
        seconds.append(second_layer(apart, pieces, layers[1], w_merge))
    placed = []
    for back_up, own_top, own_low, back_down, back_east in seconds:
        from_below = moved(back_up, "lat", -1)
        from_above = moved(back_down, "lat", 1)
        from_west = moved(back_east, "lon", 1)
        corner = moved(from_above[3:], "lon", 1)
        placed += [own_top, own_low, from_below, from_above, corner, from_west]
    rows, cols = tokens.shape[0] // 2, tokens.shape[1] // 2
    return pl.pallas_call(
        last_kernel,
        out_shape=struct(rows, cols, 4, 2 * WIDTH),
        compiler_params=pltpu.CompilerParams(vmem_limit_bytes=LIMIT),
        name="placing",
    )(*placed)


def solution(mesh):
    in_specs = (P("lat", "lon", None, None), P(), P(), P(), P())
    out_specs = P("lat", "lon", None, None)
    return jax.shard_map(body, mesh=mesh, in_specs=in_specs, out_specs=out_specs, check_vma=False)
```

profile of v0, /device:TPU:1, one launch (start us, length us, event | category | flops | bytes accessed | tf_op | source)
XLA Modules:
  0.0 161.9 jit_solution(7233840154702030512)
XLA Ops:
  0.0 1.8 %slice_bitcast_fusion = (bf16[512,1024]{1,0:T(8,128)(2,1)S(1)}, bf16[512,1024]{1,0:T(8,128)(2,1)S(1)}) fusion(bf16[2,512,1536]{2,1,0:T(8,128)(2,1)} %param.6), kind=kLoop, calls=%fused_computation | loop fusion | bytes 4194304 | tf_op jit(solution)/shard_map/squeeze | solution.py:278
  1.9 1.3 copy.9
  3.2 1.8 %slice_bitcast_fusion.2 = (bf16[512,512]{1,0:T(8,128)(2,1)S(1)}, bf16[512,512]{1,0:T(8,128)(2,1)S(1)}, bf16[512,512]{1,0:T(8,128)(2,1)S(1)}, bf16[512,512]{1,0:T(8,128)(2,1)S(1)}) fusion(bf16[2,512,512]{2,1,0:T(8,128)(2,1)} %bitcast.25, bf16[2,512,512]{2,1,0:T(8,128)(2,1)} %param.7), kind=kLoop, calls=%fused_computation.2 | loop fusion | bytes 4194304 | tf_op jit(solution)/shard_map/squeeze | solution.py:278
  5.0 0.4 copy-done
  5.5 25.9 %layer0_level2.1 = (bf16[4,72,512]{2,1,0:T(8,128)(2,1)}, bf16[4,72,512]{2,1,0:T(8,128)(2,1)S(1)}, bf16[4,72,512]{2,1,0:T(8,128)(2,1)}, bf16[3,72,512]{2,1,0:T(8,128)(2,1)S(1)}, bf16[1,72,512]{2,1,0:T(8,128)(2,1)}) custom-call(bf16[12,48,4,512]{3,2,1,0:T(4,128)(2,1)S(1)} %copy-done, bf16[512,1024]{1,0:T(8,128)(2,1)S(1)} %get-tuple-element.46.wqk_ref, ...), custom_call_target="tpu_custom_call" | custom-call | flops 7851737088 | bytes 5242880 | tf_op jit(solution)/shard_map/layer0_level2/pallas_call | solution.py:237
  31.3 0.7 copy-done.3
  32.0 0.7 copy-done.7
  32.7 9.0 %collective-permute-start.9 = (bf16[4,72,512]{2,1,0:T(8,128)(2,1)}, bf16[4,72,512]{2,1,0:T(8,128)(2,1)S(1)}, u32[]{:S(2)}, u32[]{:S(2)}) collective-permute-start(bf16[4,72,512]{2,1,0:T(8,128)(2,1)} %get-tuple-element.38), channel_id=1, source_target_pairs={{0,240},{16,0},{32,16},{48,32},{64,48},{80,64},{96,80},{112,96},{1... | collective-permute-start | bytes 884744 | tf_op jit(solution)/shard_map/ppermute | solution.py:272
  41.8 25.8 %layer0_level0.1 = (bf16[4,72,512]{2,1,0:T(8,128)(2,1)}, bf16[4,72,512]{2,1,0:T(8,128)(2,1)S(1)}, bf16[4,72,512]{2,1,0:T(8,128)(2,1)}, bf16[3,72,512]{2,1,0:T(8,128)(2,1)S(1)}, bf16[1,72,512]{2,1,0:T(8,128)(2,1)S(1)}) custom-call(bf16[12,48,4,512]{3,2,1,0:T(4,128)(2,1)S(1)} %copy-done, bf16[512,1024]{1,0:T(8,128)(2,1)S(1)} %get-tuple-element.46.wqk_ref, ...), custom_call_target="tpu_custom_call" | custom-call | flops 7851737088 | bytes 5242880 | tf_op jit(solution)/shard_map/layer0_level0/pallas_call | solution.py:237
  67.5 0.7 copy-done.1
  68.2 0.7 copy-done.5
  68.9 0.7 collective-permute-start.1
  69.6 0.7 collective-permute-start.8
  70.4 1.5 collective-permute-start.10
  71.9 1.8 %collective-permute-start.11 = (bf16[1,72,512]{2,1,0:T(8,128)(2,1)S(1)}, bf16[1,72,512]{2,1,0:T(8,128)(2,1)S(1)}, u32[]{:S(2)}, u32[]{:S(2)}) collective-permute-start(bf16[1,72,512]{2,1,0:T(8,128)(2,1)S(1)} %slice.59), channel_id=1, source_target_pairs={{0,15},{1,0},{2,1},{3,2},{4,3},{5,4},{6,5},{7,6},{8,7},{9,8},{10,9... | collective-permute-start | bytes 221192 | tf_op jit(solution)/shard_map/ppermute | solution.py:272
  73.8 2.9 %collective-permute-done.1.below_ref = bf16[4,72,512]{2,1,0:T(8,128)(2,1)S(1)} collective-permute-done((bf16[4,72,512]{2,1,0:T(8,128)(2,1)}, bf16[4,72,512]{2,1,0:T(8,128)(2,1)S(1)}, u32[]{:S(2)}, u32[]{:S(2)}) %collective-permute-start.1) | collective-permute-done | bytes 294944 | tf_op jit(solution)/shard_map/ppermute | solution.py:272
  76.7 1.9 %collective-permute-start.2 = (bf16[1,72,512]{2,1,0:T(8,128)(2,1)S(1)}, bf16[1,72,512]{2,1,0:T(8,128)(2,1)S(1)}, u32[]{:S(2)}, u32[]{:S(2)}) collective-permute-start(bf16[1,72,512]{2,1,0:T(8,128)(2,1)S(1)} %get-tuple-element.29), channel_id=1, source_target_pairs={{0,15},{1,0},{2,1},{3,2},{4,3},{5,4},{6,5},{7,6},{8,7},{9,8},{10,9... | collective-permute-start | bytes 221192 | tf_op jit(solution)/shard_map/ppermute | solution.py:272
  78.6 8.8 %collective-permute-done.10.east_low_ref = bf16[1,72,512]{2,1,0:T(8,128)(2,1)S(1)} collective-permute-done((bf16[1,72,512]{2,1,0:T(8,128)(2,1)}, bf16[1,72,512]{2,1,0:T(8,128)(2,1)S(1)}, u32[]{:S(2)}, u32[]{:S(2)}) %collective-permute-start.10) | collective-permute-done | bytes 73760 | tf_op jit(solution)/shard_map/ppermute | solution.py:272
  87.4 0.8 collective-permute-done.11.east_top_ref
  88.2 1.0 copy-done.4
  89.1 0.9 copy-done.8
  90.1 28.0 %layer1_merge.3 = (bf16[4,18,1024]{2,1,0:T(8,128)(2,1)S(1)}, bf16[4,18,1024]{2,1,0:T(8,128)(2,1)S(1)}, bf16[3,18,1024]{2,1,0:T(8,128)(2,1)S(1)}, bf16[4,18,1024]...) custom-call(f32[2]{0:T(128)S(1)} %add_select_fusion.apart_ref, bf16[4,72,512]{2,1,0:T(8,128)(2,1)S(1)} %copy-done.4, ...), custom_call_target="tpu_custom_call" | custom-call | flops 9059696640 | bytes 8388608 | tf_op jit(solution)/shard_map/layer1_merge/pallas_call | solution.py:252
  118.1 0.3 collective-permute-start.13
  118.4 27.9 %layer1_merge.2 = (bf16[4,18,1024]{2,1,0:T(8,128)(2,1)S(1)}, bf16[4,18,1024]{2,1,0:T(8,128)(2,1)S(1)}, bf16[3,18,1024]{2,1,0:T(8,128)(2,1)S(1)}, bf16[4,18,1024]...) custom-call(f32[2]{0:T(128)S(1)} %add_select_fusion.apart_ref, bf16[4,72,512]{2,1,0:T(8,128)(2,1)S(1)} %copy-done.2, ...), custom_call_target="tpu_custom_call" | custom-call | flops 9059696640 | bytes 8388608 | tf_op jit(solution)/shard_map/layer1_merge/pallas_call | solution.py:252
  146.4 5.1 %collective-permute-start.12 = (bf16[4,18,1024]{2,1,0:T(8,128)(2,1)S(1)}, bf16[4,18,1024]{2,1,0:T(8,128)(2,1)S(1)}, u32[]{:S(2)}, u32[]{:S(2)}) collective-permute-start(bf16[4,18,1024]{2,1,0:T(8,128)(2,1)S(1)} %get-tuple-element.42), channel_id=1, source_target_pairs={{0,240},{16,0},{32,16},{48,32},{64,48},{80,64},{96,80},{112,96},{1... | collective-permute-start | bytes 442376 | tf_op jit(solution)/shard_map/ppermute | solution.py:272
  151.5 1.4 collective-permute-start.4
  152.9 2.1 %collective-permute-start.15 = (bf16[1,18,1024]{2,1,0:T(8,128)(2,1)S(1)}, bf16[1,18,1024]{2,1,0:T(8,128)(2,1)S(1)}, u32[]{:S(2)}, u32[]{:S(2)}) collective-permute-start(bf16[1,18,1024]{2,1,0:T(8,128)(2,1)S(1)} %get-tuple-element.44), channel_id=1, source_target_pairs={{0,1},{1,2},{2,3},{3,4},{4,5},{5,6},{6,7},{7,8},{8,9},{9,10},{10,1... | collective-permute-start | bytes 110600 | tf_op jit(solution)/shard_map/ppermute | solution.py:272
  155.0 1.1 collective-permute-done.5.refs_3_
  156.1 0.5 collective-permute-start.14
  156.6 1.9 %collective-permute-start.6 = (bf16[1,18,1024]{2,1,0:T(8,128)(2,1)S(1)}, bf16[1,18,1024]{2,1,0:T(8,128)(2,1)S(1)}, u32[]{:S(2)}, u32[]{:S(2)}) collective-permute-start(bf16[1,18,1024]{2,1,0:T(8,128)(2,1)S(1)} %slice.58), channel_id=1, source_target_pairs={{0,1},{1,2},{2,3},{3,4},{4,5},{5,6},{6,7},{7,8},{8,9},{9,10},{10,1... | collective-permute-start | bytes 110600 | tf_op jit(solution)/shard_map/ppermute | solution.py:272
  158.5 1.7 %collective-permute-done.4.refs_2_ = bf16[4,18,1024]{2,1,0:T(8,128)(2,1)S(1)} collective-permute-done((bf16[4,18,1024]{2,1,0:T(8,128)(2,1)S(1)}, bf16[4,18,1024]{2,1,0:T(8,128)(2,1)S(1)}, u32[]{:S(2)}, u32[]{:S(2)}) %collective-permute-start.4) | collective-permute-done | bytes 147488 | tf_op jit(solution)/shard_map/ppermute | solution.py:272
  160.2 1.7 %placing.1 = bf16[6,24,4,1024]{3,2,1,0:T(4,128)(2,1)} custom-call(bf16[4,18,1024]{2,1,0:T(8,128)(2,1)S(1)} %get-tuple-element.30.refs_0_, bf16[3,18,1024]{2,1,0:T(8,128)(2,1)S(1)} %get-tuple-element.31.refs_1_, bf16[4,18,1024]{2,1,0:T(8,128)(2,1)S(1)} %collective-permute-done.4.refs_2_, bf16[4,18,1024]{2,1,0:T(8,128)(2,1)S(1)} %collective-permute-done.5.refs_3_, ...), custom_call_target="tpu_custom_call" | custom-call | tf_op jit(solution)/shard_map/placing/pallas_call | solution.py:298
  (38 shorter events, 0.3 us)
Async XLA Ops:
  0.0 1.9 %slice-start = ((bf16[2,512,1536]{2,1,0:T(8,128)(2,1)}), bf16[2,512,512]{2,1,0:T(8,128)(2,1)S(1)}, s32[]{:S(2)}) async-start(bf16[2,512,1536]{2,1,0:T(8,128)(2,1)} %param.6), calls=%async_computation | async-start | bytes 2097152 | tf_op jit(solution)/shard_map/slice | solution.py:277
  0.0 3.2 %copy-start.9 = (f32[2,3,512]{2,0,1:T(2,128)S(1)}, f32[2,3,512]{2,0,1:T(2,128)}, u32[]{:S(2)}) copy-start(f32[2,3,512]{2,0,1:T(2,128)} %param.8) | copy-start | bytes 36868
  3.2 2.3 %copy-start = (bf16[12,48,4,512]{3,2,1,0:T(4,128)(2,1)S(1)}, bf16[12,48,4,512]{3,2,1,0:T(4,128)(2,1)}, u32[]{:S(2)}) copy-start(bf16[12,48,4,512]{3,2,1,0:T(4,128)(2,1)} %tokens_ref.3) | copy-start | bytes 7077892
  31.3 0.7 copy-start.3
  32.0 0.7 copy-start.7
  32.7 39.2 %collective-permute-start.9 = (bf16[4,72,512]{2,1,0:T(8,128)(2,1)}, bf16[4,72,512]{2,1,0:T(8,128)(2,1)S(1)}, u32[]{:S(2)}, u32[]{:S(2)}) collective-permute-start(bf16[4,72,512]{2,1,0:T(8,128)(2,1)} %get-tuple-element.38), channel_id=1, source_target_pairs={{0,240},{16,0},{32,16},{48,32},{64,48},{80,64},{96,80},{112,96},{1... | collective-permute-start | bytes 884744 | tf_op jit(solution)/shard_map/ppermute | solution.py:272
  67.5 0.7 copy-start.1
  68.2 0.7 copy-start.5
  68.9 7.8 %collective-permute-start.1 = (bf16[4,72,512]{2,1,0:T(8,128)(2,1)}, bf16[4,72,512]{2,1,0:T(8,128)(2,1)S(1)}, u32[]{:S(2)}, u32[]{:S(2)}) collective-permute-start(bf16[4,72,512]{2,1,0:T(8,128)(2,1)} %get-tuple-element.28), channel_id=1, source_target_pairs={{0,240},{16,0},{32,16},{48,32},{64,48},{80,64},{96,80},{112,96},{1... | collective-permute-start | bytes 884744 | tf_op jit(solution)/shard_map/ppermute | solution.py:272
  69.6 17.7 %collective-permute-start.8 = (bf16[4,72,512]{2,1,0:T(8,128)(2,1)}, bf16[4,72,512]{2,1,0:T(8,128)(2,1)}, u32[]{:S(2)}, u32[]{:S(2)}) collective-permute-start(bf16[4,72,512]{2,1,0:T(8,128)(2,1)} %get-tuple-element.36), channel_id=1, source_target_pairs={{0,16},{16,32},{32,48},{48,64},{64,80},{80,96},{96,112},{112,128},... | collective-permute-start | bytes 884744 | tf_op jit(solution)/shard_map/ppermute | solution.py:272
  70.4 17.0 %collective-permute-start.10 = (bf16[1,72,512]{2,1,0:T(8,128)(2,1)}, bf16[1,72,512]{2,1,0:T(8,128)(2,1)S(1)}, u32[]{:S(2)}, u32[]{:S(2)}) collective-permute-start(bf16[1,72,512]{2,1,0:T(8,128)(2,1)} %get-tuple-element.39), channel_id=1, source_target_pairs={{0,15},{1,0},{2,1},{3,2},{4,3},{5,4},{6,5},{7,6},{8,7},{9,8},{10,9... | collective-permute-start | bytes 221192 | tf_op jit(solution)/shard_map/ppermute | solution.py:272
  71.9 46.5 %collective-permute-start = (bf16[4,72,512]{2,1,0:T(8,128)(2,1)}, bf16[4,72,512]{2,1,0:T(8,128)(2,1)S(1)}, u32[]{:S(2)}, u32[]{:S(2)}) collective-permute-start(bf16[4,72,512]{2,1,0:T(8,128)(2,1)} %get-tuple-element.26), channel_id=1, source_target_pairs={{0,16},{16,32},{32,48},{48,64},{64,80},{80,96},{96,112},{112,128},... | collective-permute-start | bytes 884744 | tf_op jit(solution)/shard_map/ppermute | solution.py:272
  71.9 16.2 %collective-permute-start.11 = (bf16[1,72,512]{2,1,0:T(8,128)(2,1)S(1)}, bf16[1,72,512]{2,1,0:T(8,128)(2,1)S(1)}, u32[]{:S(2)}, u32[]{:S(2)}) collective-permute-start(bf16[1,72,512]{2,1,0:T(8,128)(2,1)S(1)} %slice.59), channel_id=1, source_target_pairs={{0,15},{1,0},{2,1},{3,2},{4,3},{5,4},{6,5},{7,6},{8,7},{9,8},{10,9... | collective-permute-start | bytes 221192 | tf_op jit(solution)/shard_map/ppermute | solution.py:272
  76.7 41.7 %collective-permute-start.2 = (bf16[1,72,512]{2,1,0:T(8,128)(2,1)S(1)}, bf16[1,72,512]{2,1,0:T(8,128)(2,1)S(1)}, u32[]{:S(2)}, u32[]{:S(2)}) collective-permute-start(bf16[1,72,512]{2,1,0:T(8,128)(2,1)S(1)} %get-tuple-element.29), channel_id=1, source_target_pairs={{0,15},{1,0},{2,1},{3,2},{4,3},{5,4},{6,5},{7,6},{8,7},{9,8},{10,9... | collective-permute-start | bytes 221192 | tf_op jit(solution)/shard_map/ppermute | solution.py:272
  87.4 31.0 %collective-permute-start.3 = (bf16[1,72,512]{2,1,0:T(8,128)(2,1)S(1)}, bf16[1,72,512]{2,1,0:T(8,128)(2,1)S(1)}, u32[]{:S(2)}, u32[]{:S(2)}) collective-permute-start(bf16[1,72,512]{2,1,0:T(8,128)(2,1)S(1)} %slice.56), channel_id=1, source_target_pairs={{0,15},{1,0},{2,1},{3,2},{4,3},{5,4},{6,5},{7,6},{8,7},{9,8},{10,9... | collective-permute-start | bytes 221192 | tf_op jit(solution)/shard_map/ppermute | solution.py:272
  88.2 1.0 copy-start.4
  89.1 0.9 copy-start.8
  90.1 28.4 %copy-start.2 = (bf16[4,72,512]{2,1,0:T(8,128)(2,1)S(1)}, bf16[4,72,512]{2,1,0:T(8,128)(2,1)}, u32[]{:S(2)}) copy-start(bf16[4,72,512]{2,1,0:T(8,128)(2,1)} %copy-done.1) | copy-start | bytes 884740
  90.1 28.4 %copy-start.6 = (bf16[3,72,512]{2,1,0:T(8,128)(2,1)S(1)}, bf16[3,72,512]{2,1,0:T(8,128)(2,1)}, u32[]{:S(2)}) copy-start(bf16[3,72,512]{2,1,0:T(8,128)(2,1)} %copy-done.5) | copy-start | bytes 663556
  118.1 36.9 %collective-permute-start.13 = (bf16[4,18,1024]{2,1,0:T(8,128)(2,1)S(1)}, bf16[4,18,1024]{2,1,0:T(8,128)(2,1)S(1)}, u32[]{:S(2)}, u32[]{:S(2)}) collective-permute-start(bf16[4,18,1024]{2,1,0:T(8,128)(2,1)S(1)} %get-tuple-element.43), channel_id=1, source_target_pairs={{0,16},{16,32},{32,48},{48,64},{64,80},{80,96},{96,112},{112,128},... | collective-permute-start | bytes 442376 | tf_op jit(solution)/shard_map/ppermute | solution.py:272
  146.3 9.9 %collective-permute-start.5 = (bf16[4,18,1024]{2,1,0:T(8,128)(2,1)S(1)}, bf16[4,18,1024]{2,1,0:T(8,128)(2,1)S(1)}, u32[]{:S(2)}, u32[]{:S(2)}) collective-permute-start(bf16[4,18,1024]{2,1,0:T(8,128)(2,1)S(1)} %get-tuple-element.33), channel_id=1, source_target_pairs={{0,16},{16,32},{32,48},{48,64},{64,80},{80,96},{96,112},{112,128},... | collective-permute-start | bytes 442376 | tf_op jit(solution)/shard_map/ppermute | solution.py:272
  146.4 12.1 %collective-permute-start.12 = (bf16[4,18,1024]{2,1,0:T(8,128)(2,1)S(1)}, bf16[4,18,1024]{2,1,0:T(8,128)(2,1)S(1)}, u32[]{:S(2)}, u32[]{:S(2)}) collective-permute-start(bf16[4,18,1024]{2,1,0:T(8,128)(2,1)S(1)} %get-tuple-element.42), channel_id=1, source_target_pairs={{0,240},{16,0},{32,16},{48,32},{64,48},{80,64},{96,80},{112,96},{1... | collective-permute-start | bytes 442376 | tf_op jit(solution)/shard_map/ppermute | solution.py:272
  151.5 8.7 %collective-permute-start.4 = (bf16[4,18,1024]{2,1,0:T(8,128)(2,1)S(1)}, bf16[4,18,1024]{2,1,0:T(8,128)(2,1)S(1)}, u32[]{:S(2)}, u32[]{:S(2)}) collective-permute-start(bf16[4,18,1024]{2,1,0:T(8,128)(2,1)S(1)} %get-tuple-element.32), channel_id=1, source_target_pairs={{0,240},{16,0},{32,16},{48,32},{64,48},{80,64},{96,80},{112,96},{1... | collective-permute-start | bytes 442376 | tf_op jit(solution)/shard_map/ppermute | solution.py:272
  152.9 3.7 %collective-permute-start.15 = (bf16[1,18,1024]{2,1,0:T(8,128)(2,1)S(1)}, bf16[1,18,1024]{2,1,0:T(8,128)(2,1)S(1)}, u32[]{:S(2)}, u32[]{:S(2)}) collective-permute-start(bf16[1,18,1024]{2,1,0:T(8,128)(2,1)S(1)} %get-tuple-element.44), channel_id=1, source_target_pairs={{0,1},{1,2},{2,3},{3,4},{4,5},{5,6},{6,7},{7,8},{8,9},{9,10},{10,1... | collective-permute-start | bytes 110600 | tf_op jit(solution)/shard_map/ppermute | solution.py:272
  155.0 3.5 %collective-permute-start.7 = (bf16[1,18,1024]{2,1,0:T(8,128)(2,1)S(1)}, bf16[1,18,1024]{2,1,0:T(8,128)(2,1)S(1)}, u32[]{:S(2)}, u32[]{:S(2)}) collective-permute-start(bf16[1,18,1024]{2,1,0:T(8,128)(2,1)S(1)} %get-tuple-element.34), channel_id=1, source_target_pairs={{0,1},{1,2},{2,3},{3,4},{4,5},{5,6},{6,7},{7,8},{8,9},{9,10},{10,1... | collective-permute-start | bytes 110600 | tf_op jit(solution)/shard_map/ppermute | solution.py:272
  156.1 4.1 %collective-permute-start.14 = (bf16[1,18,1024]{2,1,0:T(8,128)(2,1)S(1)}, bf16[1,18,1024]{2,1,0:T(8,128)(2,1)S(1)}, u32[]{:S(2)}, u32[]{:S(2)}) collective-permute-start(bf16[1,18,1024]{2,1,0:T(8,128)(2,1)S(1)} %slice.60), channel_id=1, source_target_pairs={{0,1},{1,2},{2,3},{3,4},{4,5},{5,6},{6,7},{7,8},{8,9},{9,10},{10,1... | collective-permute-start | bytes 110600 | tf_op jit(solution)/shard_map/ppermute | solution.py:272
  156.6 3.6 %collective-permute-start.6 = (bf16[1,18,1024]{2,1,0:T(8,128)(2,1)S(1)}, bf16[1,18,1024]{2,1,0:T(8,128)(2,1)S(1)}, u32[]{:S(2)}, u32[]{:S(2)}) collective-permute-start(bf16[1,18,1024]{2,1,0:T(8,128)(2,1)S(1)} %slice.58), channel_id=1, source_target_pairs={{0,1},{1,2},{2,3},{3,4},{4,5},{5,6},{6,7},{7,8},{8,9},{9,10},{10,1... | collective-permute-start | bytes 110600 | tf_op jit(solution)/shard_map/ppermute | solution.py:272
where the time goes:
time: 163 us; the launch traced here: 162 us
  Pallas kernels  109 us (67%)
  starting transfers between devices  27.1 us (17%)
  waiting for transfers between devices  15.3 us (9%)
  local copies, waits for them, and re-layouts  10.1 us (6%)
    pallas_call x2, Pallas kernels, second_layer(): pl.pallas_call(second_kernel, grid=(4,), in_specs=[pl.BlockSpec(memory_sp...  55.9 us
    pallas_call x2, Pallas kernels, first_layer(): pl.pallas_call(functools.partial(first_kernel, level), grid=(4,), in_spec...  51.6 us
    ppermute x16, starting transfers between devices, moved(): lax.ppermute(value, axis, [(source, (source + steps) % count) for source...  27.1 us
    ppermute x16, waiting for transfers between devices, moved(): lax.ppermute(value, axis, [(source, (source + steps) % count) for source...  15.3 us
    unnamed x23, local copies, waits for them, and re-layouts  6.43 us
    squeeze x2, local copies, waits for them, and re-layouts, body(): layers = [(wqk[i], wvt[i], w_out[i], modulation[i]) for i in range(2)]  3.63 us
  transfers between devices with their start and end apart: 16, of which 5 were waited for; matrix products, arithmetic and copies ran while one was open for 0% of the time, Pallas kernels for 50%

commit v1 on v0

v1 whole, which is shorter than its diff:
```python
import functools
import math

import jax
import jax.numpy as jnp
from jax import lax
from jax.experimental import pallas as pl
from jax.experimental.pallas import tpu as pltpu
from jax.sharding import PartitionSpec as P

HEADS = 16
WIN = 12
HALF = 6
QUAD = 72
SPAN = 4 * QUAD
WIDTH = 512
HEAD = WIDTH // HEADS
GROUP = 8
MAIN = 256
REST = SPAN - MAIN
SUB = 18
WINDOWS = 4
FAR = -1e30
SCALE = math.log2(math.e) / math.sqrt(HEAD)
NT = (((1,), (1,)), ((), ()))


def dot(a, b):
    return jnp.dot(a, b, preferred_element_type=jnp.float32)


def dot_nt(a, b):
    return lax.dot_general(a, b, NT, preferred_element_type=jnp.float32)


def normalized(values, eps):
    centered = values - jnp.mean(values, axis=-1, keepdims=True)
    return centered * lax.rsqrt(jnp.mean(centered * centered, axis=-1, keepdims=True) + eps)


def softened(scores, apart, straddles):
    half = SPAN // 2
    top, bottom = scores[:half], scores[half:]
    if apart is None:
        most = jnp.maximum(jnp.max(top, axis=0, keepdims=True), jnp.max(bottom, axis=0, keepdims=True))
        return jnp.exp2(scores - most).astype(jnp.bfloat16)
    if straddles:
        lane = lax.broadcasted_iota(jnp.int32, (1, MAIN), 1)
        from_top = jnp.where(lane < half, 0.0, apart)
        from_bottom = jnp.where(lane < half, apart, 0.0)
    else:
        from_top = jnp.full((1, MAIN), apart, jnp.float32)
        from_bottom = jnp.zeros((1, MAIN), jnp.float32)
    most = jnp.maximum(
        jnp.max(top, axis=0, keepdims=True) + from_top, jnp.max(bottom, axis=0, keepdims=True) + from_bottom
    )
    return jnp.concatenate(
        [
            jnp.exp2(top - (most - from_top)).astype(jnp.bfloat16),
            jnp.exp2(bottom - (most - from_bottom)).astype(jnp.bfloat16),
        ],
        axis=0,
    )


def attend_windows(grid_ref, wqkv_ref, wout_ref, mod_ref, scratch, aparts):
    hidden_ref, query_ref, keys_ref, vt_ref, scores_ref, rest_ref, att_ref = scratch
    wide = GROUP * HEAD
    lane_head = lax.broadcasted_iota(jnp.int32, (1, wide), 1) // HEAD
    same = (
        lax.broadcasted_iota(jnp.int32, (wide, wide), 0) // HEAD
        == lax.broadcasted_iota(jnp.int32, (wide, wide), 1) // HEAD
    )
    fold = (
        lax.broadcasted_iota(jnp.int32, (REST, wide), 0) == lax.broadcasted_iota(jnp.int32, (REST, wide), 1) % HEAD
    ).astype(jnp.bfloat16)
    ones = jnp.ones((16, SPAN), jnp.bfloat16)

    def main_rows(w):
        return pl.ds(pl.multiple_of(w * MAIN, MAIN), MAIN)

    def rest_rows(w):
        return pl.ds(pl.multiple_of(WINDOWS * MAIN + w * REST, REST), REST)

    @pl.loop(0, WINDOWS)
    def _(w):
        hidden = (normalized(grid_ref[w], 1e-06) * (1.0 + mod_ref[0:1]) + mod_ref[1:2]).astype(jnp.bfloat16)
        hidden_ref[main_rows(w)] = hidden[:MAIN]
        hidden_ref[rest_rows(w)] = hidden[MAIN:]

    query_ref[...] = (dot(hidden_ref[...], wqkv_ref[:, :WIDTH]) * SCALE).astype(jnp.bfloat16)
    keys_ref[...] = dot(hidden_ref[...], wqkv_ref[:, WIDTH : 2 * WIDTH]).astype(jnp.bfloat16)
    values = dot_nt(wqkv_ref[:, 2 * WIDTH :].T, hidden_ref[...]).astype(jnp.bfloat16)
    for w in range(WINDOWS):
        vt_ref[w, :, :MAIN] = values[:, w * MAIN : (w + 1) * MAIN]
        vt_ref[w, :, MAIN:] = values[:, WINDOWS * MAIN + w * REST : WINDOWS * MAIN + (w + 1) * REST]

    @pl.loop(0, WINDOWS)
    def _(w):
        apart = None if aparts is None else jnp.where(w < 2, aparts[0], aparts[1])
        for group in range(HEADS // GROUP):
            cols = slice(group * wide, (group + 1) * wide)
            kg = jnp.concatenate([keys_ref[main_rows(w), cols], keys_ref[rest_rows(w), cols]], axis=0)
            qm, qr = query_ref[main_rows(w), cols], query_ref[rest_rows(w), cols]
            for part in range(2):
                items = range(part * GROUP // 2, (part + 1) * GROUP // 2)
                masked = jnp.concatenate([kg * (lane_head == item).astype(jnp.bfloat16) for item in items], axis=0)
                scores_ref[2 * group + part] = dot_nt(masked, qm)
            rest_ref[group] = dot_nt(kg, jnp.concatenate([qr] * GROUP, axis=0) * same.astype(jnp.bfloat16))
        rest = []
        for group in range(HEADS // GROUP):
            cols = slice(group * wide, (group + 1) * wide)
            for item in range(GROUP):
                heads = slice((group * GROUP + item) * HEAD, (group * GROUP + item + 1) * HEAD)
                start = item % (GROUP // 2) * SPAN
                scores = scores_ref[2 * group + item // (GROUP // 2), start : start + SPAN]
                weights = softened(scores, apart, True)
                mixed = dot(jnp.concatenate([vt_ref[w, heads], ones], axis=0), weights)
                att_ref[heads] = mixed[:HEAD] * (1.0 / mixed[HEAD : HEAD + 1])
            weights = softened(rest_ref[group], apart, False)
            mixed = dot(jnp.concatenate([vt_ref[w, cols], ones], axis=0), weights)
            mixed = jnp.where(same, mixed[:wide] * (1.0 / mixed[wide : wide + 1]), 0.0).astype(jnp.bfloat16)
            rest.append(dot_nt(fold, mixed).astype(jnp.bfloat16))
        hidden_ref[main_rows(w)] = att_ref[...].T.astype(jnp.bfloat16)
        hidden_ref[rest_rows(w)] = jnp.concatenate(rest, axis=1)

    added = (1.0 + mod_ref[2:3]) * dot(hidden_ref[...], wout_ref[...])
    for w in range(WINDOWS):
        grid_ref[w, :MAIN] += added[w * MAIN : (w + 1) * MAIN]
        grid_ref[w, MAIN:] += added[WINDOWS * MAIN + w * REST : WINDOWS * MAIN + (w + 1) * REST]


def first_kernel(
    level, tokens_ref, wqkv_ref, wout_ref, mod_ref, up_ref, corner_ref, stay_top_ref, down_ref, stay_low_ref, west_ref,
    grid_ref, *scratch,
):
    @pl.loop(0, WINDOWS)
    def _(w):
        for quad in range(4):
            for sub in range(4):
                for place in range(9):
                    i = quad // 2 * HALF + place // 3 * 2 + sub % 2
                    j = quad % 2 * HALF + place % 3 * 2 + sub // 2
                    row = quad * QUAD + sub * SUB + place * 2
                    grid_ref[w, row : row + 2] = tokens_ref[i, w * WIN + j, level : level + 2].astype(jnp.float32)

    attend_windows(grid_ref, wqkv_ref.at[0], wout_ref.at[0], mod_ref.at[0], scratch, None)
    for block in range(8):
        w, side = divmod(block, 2)
        top = grid_ref[w, side * QUAD : (side + 1) * QUAD].astype(jnp.bfloat16)
        low = grid_ref[w, (2 + side) * QUAD : (3 + side) * QUAD].astype(jnp.bfloat16)
        if 1 <= block <= 4:
            stay_top_ref[block - 1] = top
            down_ref[block - 1] = low
        else:
            (up_ref if block else corner_ref)[max(block - 5, 0)] = top
            (stay_low_ref if block else west_ref)[max(block - 5, 0)] = low


def second_kernel(
    apart_ref, stay_top_ref, above_ref, stay_low_ref, below_ref, east_low_ref, east_top_ref,
    wqkv_ref, wout_ref, mod_ref, merge_ref,
    back_up_ref, own_top_ref, own_low_ref, back_down_ref, back_east_ref, back_corner_ref,
    grid_ref, *scratch,
):
    *scratch, joined_ref = scratch
    sources = [
        [(above_ref, 0), (above_ref, 1), (stay_top_ref, 0), (stay_top_ref, 1)],
        [(above_ref, 2), (above_ref, 3), (stay_top_ref, 2), (stay_top_ref, 3)],
        [(stay_low_ref, 0), (stay_low_ref, 1), (below_ref, 0), (below_ref, 1)],
        [(stay_low_ref, 2), (east_low_ref, 0), (below_ref, 2), (east_top_ref, 0)],
    ]
    for w in range(WINDOWS):
        for quad, (ref, index) in enumerate(sources[w]):
            grid_ref[w, quad * QUAD : (quad + 1) * QUAD] = ref[index].astype(jnp.float32)
    aparts = (apart_ref[0], apart_ref[1])
    attend_windows(grid_ref, wqkv_ref.at[1], wout_ref.at[1], mod_ref.at[1], scratch, aparts)

    @pl.loop(0, WINDOWS)
    def _(w):
        for quad in range(4):
            for sub in range(4):
                start = quad * QUAD + sub * SUB
                joined_ref[w, quad * SUB : (quad + 1) * SUB, sub * WIDTH : (sub + 1) * WIDTH] = (
                    grid_ref[w, start : start + SUB].astype(jnp.bfloat16).astype(jnp.float32)
                )

    flat = jnp.concatenate([normalized(joined_ref[w], 1e-05).astype(jnp.bfloat16) for w in range(WINDOWS)], axis=0)
    merged = dot(flat, merge_ref[...])

    def piece(w, quad):
        return merged[w * QUAD + quad * SUB : w * QUAD + (quad + 1) * SUB].astype(jnp.bfloat16)

    for w in range(2):
        for side in range(2):
            back_up_ref[2 * w + side] = piece(w, side)
            own_top_ref[2 * w + side] = piece(w, 2 + side)
    own_low_ref[0], own_low_ref[1], own_low_ref[2] = piece(2, 0), piece(2, 1), piece(3, 0)
    back_down_ref[0], back_down_ref[1], back_down_ref[2] = piece(2, 2), piece(2, 3), piece(3, 2)
    back_east_ref[0], back_corner_ref[0] = piece(3, 1), piece(3, 3)


def last_kernel(*refs):
    out_ref = refs[-1]
    for pair in range(2):
        own_top, own_low, from_below, from_above, corner, from_west = refs[6 * pair : 6 * pair + 6]
        sources = {(0, 0): (corner, 0), (1, 0): (from_west, 0)}
        for c in range(4):
            sources[0, c + 1], sources[1, c + 1] = (own_top, c), (from_below, c)
        for c in range(3):
            sources[0, c + 5], sources[1, c + 5] = (from_above, c), (own_low, c)
        for (half, block), (ref, index) in sources.items():
            for place in range(9):
                i, j = half * 3 + place // 3, block * 3 + place % 3
                out_ref[i, j, 2 * pair : 2 * pair + 2] = ref[index, 2 * place : 2 * place + 2]


def whole(*shape):
    return pl.BlockSpec(shape, lambda: (0,) * len(shape))


def struct(*shape):
    return jax.ShapeDtypeStruct(shape, jnp.bfloat16)


LIMIT = 28 * 1024 * 1024
LAYER_SCRATCH = [
    pltpu.VMEM((WINDOWS, SPAN, WIDTH), jnp.float32),
    pltpu.VMEM((WINDOWS * SPAN, WIDTH), jnp.bfloat16),
    pltpu.VMEM((WINDOWS * SPAN, WIDTH), jnp.bfloat16),
    pltpu.VMEM((WINDOWS * SPAN, WIDTH), jnp.bfloat16),
    pltpu.VMEM((WINDOWS, WIDTH, SPAN), jnp.bfloat16),
    pltpu.VMEM((4, HEADS // 4 * SPAN, MAIN), jnp.float32),
    pltpu.VMEM((HEADS // GROUP, SPAN, MAIN), jnp.float32),
    pltpu.VMEM((WIDTH, MAIN), jnp.float32),
]


LAYER_SPECS = [whole(2, WIDTH, 3 * WIDTH), whole(2, WIDTH, WIDTH), whole(2, 3, WIDTH)]
LAYER_FLOPS = 2 * 4 * SPAN * (4 * WIDTH * WIDTH + 2 * 8 * SPAN * WIDTH)


def first_layer(level, tokens, layers):
    counts = (3, 1, 4, 4, 3, 1)
    return pl.pallas_call(
        functools.partial(first_kernel, level),
        in_specs=[whole(*tokens.shape)] + LAYER_SPECS,
        out_specs=[whole(n, QUAD, WIDTH) for n in counts],
        out_shape=[struct(n, QUAD, WIDTH) for n in counts],
        scratch_shapes=LAYER_SCRATCH,
        compiler_params=pltpu.CompilerParams(vmem_limit_bytes=LIMIT),
        cost_estimate=pl.CostEstimate(flops=LAYER_FLOPS, bytes_accessed=5 << 20, transcendentals=16 * 4 * SPAN * SPAN),
        name=f"layer0_level{level}",
    )(tokens, *layers)


def second_layer(apart, pieces, layers, w_merge):
    outs = (4, 4, 3, 3, 1, 1)
    return pl.pallas_call(
        second_kernel,
        in_specs=[pl.BlockSpec(memory_space=pltpu.SMEM)]
        + [whole(p.shape[0], QUAD, WIDTH) for p in pieces]
        + LAYER_SPECS
        + [whole(4 * WIDTH, 2 * WIDTH)],
        out_specs=[whole(n, SUB, 2 * WIDTH) for n in outs],
        out_shape=[struct(n, SUB, 2 * WIDTH) for n in outs],
        scratch_shapes=LAYER_SCRATCH + [pltpu.VMEM((4, QUAD, 4 * WIDTH), jnp.float32)],
        compiler_params=pltpu.CompilerParams(vmem_limit_bytes=LIMIT),
        cost_estimate=pl.CostEstimate(
            flops=LAYER_FLOPS + 2 * SPAN * 8 * WIDTH * WIDTH, bytes_accessed=8 << 20, transcendentals=16 * 4 * SPAN * SPAN
        ),
        name="layer1_merge",
    )(apart, *pieces, *layers, w_merge)


def moved(value, down, east):
    lats, lons = lax.axis_size("lat"), lax.axis_size("lon")
    pairs = [
        (lat * lons + lon, (lat + down) % lats * lons + (lon + east) % lons) for lat in range(lats) for lon in range(lons)
    ]
    return lax.ppermute(value, ("lat", "lon"), pairs)


def body(tokens, w_qkv, w_out, modulation, w_merge):
    layers = (w_qkv, w_out, modulation)
    lat, last = lax.axis_index("lat"), lax.axis_size("lat") - 1
    apart = jnp.where(jnp.stack([lat == 0, lat == last]), FAR, 0.0).astype(jnp.float32)
    firsts = [first_layer(level, tokens, layers) for level in (0, 2)]
    seconds = []
    for up, corner, stay_top, down, stay_low, west in firsts:
        pieces = (stay_top, moved(down, 1, 0), stay_low, moved(up, -1, 0), moved(west, 0, -1), moved(corner, -1, -1))
        seconds.append(second_layer(apart, pieces, layers, w_merge))
    placed = []
    for back_up, own_top, own_low, back_down, back_east, back_corner in seconds:
        placed += [
            own_top, own_low, moved(back_up, -1, 0), moved(back_down, 1, 0), moved(back_corner, 1, 1), moved(back_east, 0, 1)
        ]
    rows, cols = tokens.shape[0] // 2, tokens.shape[1] // 2
    return pl.pallas_call(
        last_kernel,
        out_shape=struct(rows, cols, 4, 2 * WIDTH),
        compiler_params=pltpu.CompilerParams(vmem_limit_bytes=LIMIT),
        name="placing",
    )(*placed)


def solution(mesh):
    in_specs = (P("lat", "lon", None, None), P(), P(), P(), P())
    out_specs = P("lat", "lon", None, None)
    return jax.shard_map(body, mesh=mesh, in_specs=in_specs, out_specs=out_specs, check_vma=False)
```

time: 163 us -> 121 us (0.74)
  Pallas kernels: 109 us -> 58.6 us
  local copies, waits for them, and re-layouts: 10.1 us -> 14.9 us
  starting transfers between devices: 27.1 us -> 31.7 us
  waiting for transfers between devices: 15.3 us -> 13.2 us
    pallas_call x4, Pallas kernels: 107 us -> 56.9 us  [the longest x2 29.6 us: second_layer(): pl.pallas_call(second_kernel, in_specs=[pl.BlockSpec(memory_space=pltpu.S...]
    unnamed x23 -> x35, local copies, waits for them, and re-layouts: 6.43 us -> 14.9 us
    ppermute x16, starting transfers between devices: 27.1 us -> 31.7 us  [moved(): return lax.ppermute(value, ('lat', 'lon'), pairs)]
    squeeze x2 -> x0, local copies, waits for them, and re-layouts: 3.63 us -> none  [body(): layers = [(wqk[i], wvt[i], w_out[i], modulation[i]) for i in range(2)]]
    ppermute x16, waiting for transfers between devices: 15.3 us -> 13.2 us  [moved(): return lax.ppermute(value, ('lat', 'lon'), pairs)]
  transfers between devices with their start and end apart: 16 -> 16, of which waited for: 5 -> 2; matrix products, arithmetic and copies ran while one was open for 0% -> 0% of each run, Pallas kernels for 50% -> 36%
where the time goes in v1:
time: 121 us; the launch traced here: 119 us
  Pallas kernels  58.6 us (48%)
  starting transfers between devices  31.7 us (26%)
  local copies, waits for them, and re-layouts  14.9 us (12%)
  waiting for transfers between devices  13.2 us (11%)
    ppermute x16, starting transfers between devices, moved(): return lax.ppermute(value, ('lat', 'lon'), pairs)  31.7 us
    pallas_call x2, Pallas kernels, second_layer(): pl.pallas_call(second_kernel, in_specs=[pl.BlockSpec(memory_space=pltpu.S...  29.6 us
    pallas_call x2, Pallas kernels, first_layer(): pl.pallas_call(functools.partial(first_kernel, level), in_specs=[whole(*t...  27.3 us
    unnamed x35, local copies, waits for them, and re-layouts  14.9 us
    ppermute x16, waiting for transfers between devices, moved(): return lax.ppermute(value, ('lat', 'lon'), pairs)  13.2 us
  transfers between devices with their start and end apart: 16, of which 2 were waited for; matrix products, arithmetic and copies ran while one was open for 0% of the time, Pallas kernels for 36%

profile of v1, /device:TPU:1, one launch (start us, length us, event | category | flops | bytes accessed | tf_op | source)
XLA Modules:
  0.0 118.6 jit_solution(11551329775291067726)
XLA Ops:
  0.0 0.7 copy.6.mod_ref
  0.7 1.9 %copy-done.2 = bf16[2,512,1536]{2,1,0:T(8,128)(2,1)S(1)} copy-done((bf16[2,512,1536]{2,1,0:T(8,128)(2,1)S(1)}, bf16[2,512,1536]{2,1,0:T(8,128)(2,1)}, u32[]{:S(2)}) %copy-start.2) | copy-done | bytes 3145752
  2.6 1.7 %copy-done.4 = bf16[12,48,4,512]{3,2,1,0:T(4,128)(2,1)S(1)} copy-done((bf16[12,48,4,512]{3,2,1,0:T(4,128)(2,1)S(1)}, bf16[12,48,4,512]{3,2,1,0:T(4,128)(2,1)}, u32[]{:S(2)}) %copy-start.4) | copy-done | bytes 2359320
  4.3 1.2 %copy-done.5 = bf16[2,512,512]{2,1,0:T(8,128)(2,1)S(1)} copy-done((bf16[2,512,512]{2,1,0:T(8,128)(2,1)S(1)}, bf16[2,512,512]{2,1,0:T(8,128)(2,1)}, u32[]{:S(2)}) %copy-start.5) | copy-done | bytes 1048600
  5.5 13.8 %layer0_level2.1 = (bf16[3,72,512]{2,1,0:T(8,128)(2,1)}, bf16[1,72,512]{2,1,0:T(8,128)(2,1)}, bf16[4,72,512]{2,1,0:T(8,128)(2,1)S(1)}, bf16[4,72,512]{2,1,0:T(8,...) custom-call(bf16[12,48,4,512]{3,2,1,0:T(4,128)(2,1)S(1)} %copy-done.4, ...), custom_call_target="tpu_custom_call" | custom-call | flops 7851737088 | bytes 5242880 | tf_op jit(solution)/shard_map/layer0_level2/pallas_call | solution.py:245
  19.3 0.7 copy-done.11
  20.0 0.7 copy-done.15
  20.7 3.2 %collective-permute-start.10 = (bf16[1,72,512]{2,1,0:T(8,128)(2,1)}, bf16[1,72,512]{2,1,0:T(8,128)(2,1)}, u32[]{:S(2)}, u32[]{:S(2)}) collective-permute-start(bf16[1,72,512]{2,1,0:T(8,128)(2,1)} %get-tuple-element.45), channel_id=1, source_target_pairs={{0,15},{1,0},{2,1},{3,2},{4,3},{5,4},{6,5},{7,6},{8,7},{9,8},{10,9... | collective-permute-start | bytes 221192 | tf_op jit(solution)/shard_map/ppermute | solution.py:281
  24.0 9.3 %collective-permute-start.11 = (bf16[1,72,512]{2,1,0:T(8,128)(2,1)}, bf16[1,72,512]{2,1,0:T(8,128)(2,1)}, u32[]{:S(2)}, u32[]{:S(2)}) collective-permute-start(bf16[1,72,512]{2,1,0:T(8,128)(2,1)} %get-tuple-element.46), channel_id=1, source_target_pairs={{0,255},{1,240},{2,241},{3,242},{4,243},{5,244},{6,245},{7,246},{8... | collective-permute-start | bytes 221192 | tf_op jit(solution)/shard_map/ppermute | solution.py:281
  33.2 0.7 collective-permute-start.9
  33.9 0.7 collective-permute-start.8
  34.7 13.4 %layer0_level0.1 = (bf16[3,72,512]{2,1,0:T(8,128)(2,1)S(1)}, bf16[1,72,512]{2,1,0:T(8,128)(2,1)S(1)}, bf16[4,72,512]{2,1,0:T(8,128)(2,1)S(1)}, bf16[4,72,512]{2,...) custom-call(bf16[12,48,4,512]{3,2,1,0:T(4,128)(2,1)S(1)} %copy-done.4, ...), custom_call_target="tpu_custom_call" | custom-call | flops 7851737088 | bytes 5242880 | tf_op jit(solution)/shard_map/layer0_level0/pallas_call | solution.py:245
  48.1 0.7 copy-done.7
  48.8 0.6 copy-done.8
  49.4 0.7 copy-done.9
  50.2 0.7 copy-done.13
  51.1 5.1 %collective-permute-start.3 = (bf16[1,72,512]{2,1,0:T(8,128)(2,1)}, bf16[1,72,512]{2,1,0:T(8,128)(2,1)S(1)}, u32[]{:S(2)}, u32[]{:S(2)}) collective-permute-start(bf16[1,72,512]{2,1,0:T(8,128)(2,1)} %copy-done.8), channel_id=1, source_target_pairs={{0,255},{1,240},{2,241},{3,242},{4,243},{5,244},{6,245},{7,246},{8... | collective-permute-start | bytes 221192 | tf_op jit(solution)/shard_map/ppermute | solution.py:281
  56.2 0.2 collective-permute-start.1
  56.5 1.3 %collective-permute-start = (bf16[4,72,512]{2,1,0:T(8,128)(2,1)S(1)}, bf16[4,72,512]{2,1,0:T(8,128)(2,1)S(1)}, u32[]{:S(2)}, u32[]{:S(2)}) collective-permute-start(bf16[4,72,512]{2,1,0:T(8,128)(2,1)S(1)} %get-tuple-element.30), channel_id=1, source_target_pairs={{0,16},{1,17},{2,18},{3,19},{4,20},{5,21},{6,22},{7,23},{8,24},{9,... | collective-permute-start | bytes 884744 | tf_op jit(solution)/shard_map/ppermute | solution.py:281
  57.7 2.2 %copy-done = bf16[2048,1024]{1,0:T(8,128)(2,1)S(1)} copy-done((bf16[2048,1024]{1,0:T(8,128)(2,1)S(1)}, bf16[2048,1024]{1,0:T(8,128)(2,1)}, u32[]{:S(2)}) %copy-start) | copy-done | bytes 4194328
  59.9 1.2 %copy-done.6 = bf16[2,512,512]{2,1,0:T(8,128)(2,1)S(1)} copy-done((bf16[2,512,512]{2,1,0:T(8,128)(2,1)S(1)}, bf16[2,512,512]{2,1,0:T(8,128)(2,1)}, u32[]{:S(2)}) %copy-start.6) | copy-done | bytes 1048600
  61.1 1.0 copy-done.12
  62.1 0.9 copy-done.16
  63.0 15.2 %layer1_merge.3 = (bf16[4,18,1024]{2,1,0:T(8,128)(2,1)S(1)}, bf16[4,18,1024]{2,1,0:T(8,128)(2,1)S(1)}, bf16[3,18,1024]{2,1,0:T(8,128)(2,1)S(1)}, bf16[3,18,1024]...) custom-call(f32[2]{0:T(128)S(1)} %add_select_fusion.apart_ref, ...), custom_call_target="tpu_custom_call" | custom-call | flops 9059696640 | bytes 8388608 | tf_op jit(solution)/shard_map/layer1_merge/pallas_call | solution.py:259
  78.4 4.5 %collective-permute-start.12 = (bf16[4,18,1024]{2,1,0:T(8,128)(2,1)S(1)}, bf16[4,18,1024]{2,1,0:T(8,128)(2,1)S(1)}, u32[]{:S(2)}, u32[]{:S(2)}) collective-permute-start(bf16[4,18,1024]{2,1,0:T(8,128)(2,1)S(1)} %get-tuple-element.49), channel_id=1, source_target_pairs={{0,240},{1,241},{2,242},{3,243},{4,244},{5,245},{6,246},{7,247},{8... | collective-permute-start | bytes 442376 | tf_op jit(solution)/shard_map/ppermute | solution.py:281
  82.9 14.5 %layer1_merge.2 = (bf16[4,18,1024]{2,1,0:T(8,128)(2,1)S(1)}, bf16[4,18,1024]{2,1,0:T(8,128)(2,1)S(1)}, bf16[3,18,1024]{2,1,0:T(8,128)(2,1)S(1)}, bf16[3,18,1024]...) custom-call(f32[2]{0:T(128)S(1)} %add_select_fusion.apart_ref, ...), custom_call_target="tpu_custom_call" | custom-call | flops 9059696640 | bytes 8388608 | tf_op jit(solution)/shard_map/layer1_merge/pallas_call | solution.py:259
  97.3 1.8 %collective-permute-start.4 = (bf16[4,18,1024]{2,1,0:T(8,128)(2,1)S(1)}, bf16[4,18,1024]{2,1,0:T(8,128)(2,1)S(1)}, u32[]{:S(2)}, u32[]{:S(2)}) collective-permute-start(bf16[4,18,1024]{2,1,0:T(8,128)(2,1)S(1)} %get-tuple-element.37), channel_id=1, source_target_pairs={{0,240},{1,241},{2,242},{3,243},{4,244},{5,245},{6,246},{7,247},{8... | collective-permute-start | bytes 442376 | tf_op jit(solution)/shard_map/ppermute | solution.py:281
  99.3 1.1 collective-permute-start.13
  100.5 3.2 %collective-permute-start.6 = (bf16[1,18,1024]{2,1,0:T(8,128)(2,1)S(1)}, bf16[1,18,1024]{2,1,0:T(8,128)(2,1)S(1)}, u32[]{:S(2)}, u32[]{:S(2)}) collective-permute-start(bf16[1,18,1024]{2,1,0:T(8,128)(2,1)S(1)} %get-tuple-element.39), channel_id=1, source_target_pairs={{0,17},{1,18},{2,19},{3,20},{4,21},{5,22},{6,23},{7,24},{8,25},{9,... | collective-permute-start | bytes 110600 | tf_op jit(solution)/shard_map/ppermute | solution.py:281
  103.7 9.0 %collective-permute-done.6.refs_4_ = bf16[1,18,1024]{2,1,0:T(8,128)(2,1)S(1)} collective-permute-done((bf16[1,18,1024]{2,1,0:T(8,128)(2,1)S(1)}, bf16[1,18,1024]{2,1,0:T(8,128)(2,1)S(1)}, u32[]{:S(2)}, u32[]{:S(2)}) %collective-permute-start.6) | collective-permute-done | bytes 36896 | tf_op jit(solution)/shard_map/ppermute | solution.py:281
  112.7 4.2 %collective-permute-done.7.refs_5_ = bf16[1,18,1024]{2,1,0:T(8,128)(2,1)S(1)} collective-permute-done((bf16[1,18,1024]{2,1,0:T(8,128)(2,1)S(1)}, bf16[1,18,1024]{2,1,0:T(8,128)(2,1)S(1)}, u32[]{:S(2)}, u32[]{:S(2)}) %collective-permute-start.7) | collective-permute-done | bytes 36896 | tf_op jit(solution)/shard_map/ppermute | solution.py:281
  116.9 1.7 %placing.1 = bf16[6,24,4,1024]{3,2,1,0:T(4,128)(2,1)} custom-call(bf16[4,18,1024]{2,1,0:T(8,128)(2,1)S(1)} %get-tuple-element.35.refs_0_, bf16[3,18,1024]{2,1,0:T(8,128)(2,1)S(1)} %get-tuple-element.36.refs_1_, bf16[4,18,1024]{2,1,0:T(8,128)(2,1)S(1)} %collective-permute-done.4.refs_2_, bf16[3,18,1024]{2,1,0:T(8,128)(2,1)S(1)} %collective-permute-done.5.refs_3_, ...), custom_call_target="tpu_custom_call" | custom-call | tf_op jit(solution)/shard_map/placing/pallas_call | solution.py:299
  (41 shorter events, 0.7 us)
Async XLA Ops:
  0.7 1.9 %copy-start.2 = (bf16[2,512,1536]{2,1,0:T(8,128)(2,1)S(1)}, bf16[2,512,1536]{2,1,0:T(8,128)(2,1)}, u32[]{:S(2)}) copy-start(bf16[2,512,1536]{2,1,0:T(8,128)(2,1)} %wqkv_ref.7) | copy-start | bytes 9437188
  2.6 1.7 %copy-start.4 = (bf16[12,48,4,512]{3,2,1,0:T(4,128)(2,1)S(1)}, bf16[12,48,4,512]{3,2,1,0:T(4,128)(2,1)}, u32[]{:S(2)}) copy-start(bf16[12,48,4,512]{3,2,1,0:T(4,128)(2,1)} %tokens_ref.3) | copy-start | bytes 7077892
  4.3 1.2 %copy-start.5 = (bf16[2,512,512]{2,1,0:T(8,128)(2,1)S(1)}, bf16[2,512,512]{2,1,0:T(8,128)(2,1)}, u32[]{:S(2)}) copy-start(bf16[2,512,512]{2,1,0:T(8,128)(2,1)} %wout_ref.7) | copy-start | bytes 3145732
  19.3 0.7 copy-start.11
  20.0 0.7 copy-start.15
  20.7 30.4 %collective-permute-start.10 = (bf16[1,72,512]{2,1,0:T(8,128)(2,1)}, bf16[1,72,512]{2,1,0:T(8,128)(2,1)}, u32[]{:S(2)}, u32[]{:S(2)}) collective-permute-start(bf16[1,72,512]{2,1,0:T(8,128)(2,1)} %get-tuple-element.45), channel_id=1, source_target_pairs={{0,15},{1,0},{2,1},{3,2},{4,3},{5,4},{6,5},{7,6},{8,7},{9,8},{10,9... | collective-permute-start | bytes 221192 | tf_op jit(solution)/shard_map/ppermute | solution.py:281
  24.0 32.3 %collective-permute-start.11 = (bf16[1,72,512]{2,1,0:T(8,128)(2,1)}, bf16[1,72,512]{2,1,0:T(8,128)(2,1)}, u32[]{:S(2)}, u32[]{:S(2)}) collective-permute-start(bf16[1,72,512]{2,1,0:T(8,128)(2,1)} %get-tuple-element.46), channel_id=1, source_target_pairs={{0,255},{1,240},{2,241},{3,242},{4,243},{5,244},{6,245},{7,246},{8... | collective-permute-start | bytes 221192 | tf_op jit(solution)/shard_map/ppermute | solution.py:281
  33.2 23.2 %collective-permute-start.9 = (bf16[3,72,512]{2,1,0:T(8,128)(2,1)}, bf16[3,72,512]{2,1,0:T(8,128)(2,1)}, u32[]{:S(2)}, u32[]{:S(2)}) collective-permute-start(bf16[3,72,512]{2,1,0:T(8,128)(2,1)} %get-tuple-element.44), channel_id=1, source_target_pairs={{0,240},{1,241},{2,242},{3,243},{4,244},{5,245},{6,246},{7,247},{8... | collective-permute-start | bytes 663560 | tf_op jit(solution)/shard_map/ppermute | solution.py:281
  33.9 23.8 %copy-start.3 = (bf16[2,512,1536]{2,1,0:T(8,128)(2,1)S(1)}, bf16[2,512,1536]{2,1,0:T(8,128)(2,1)}, u32[]{:S(2)}) copy-start(bf16[2,512,1536]{2,1,0:T(8,128)(2,1)} %wqkv_ref.7) | copy-start | bytes 9437188
  33.9 23.8 %collective-permute-start.8 = (bf16[4,72,512]{2,1,0:T(8,128)(2,1)}, bf16[4,72,512]{2,1,0:T(8,128)(2,1)}, u32[]{:S(2)}, u32[]{:S(2)}) collective-permute-start(bf16[4,72,512]{2,1,0:T(8,128)(2,1)} %get-tuple-element.42), channel_id=1, source_target_pairs={{0,16},{1,17},{2,18},{3,19},{4,20},{5,21},{6,22},{7,23},{8,24},{9,... | collective-permute-start | bytes 884744 | tf_op jit(solution)/shard_map/ppermute | solution.py:281
  48.1 0.7 copy-start.7
  49.4 0.7 copy-start.9
  50.2 0.7 copy-start.13
  50.8 27.5 %collective-permute-start.2 = (bf16[1,72,512]{2,1,0:T(8,128)(2,1)}, bf16[1,72,512]{2,1,0:T(8,128)(2,1)S(1)}, u32[]{:S(2)}, u32[]{:S(2)}) collective-permute-start(bf16[1,72,512]{2,1,0:T(8,128)(2,1)} %get-tuple-element.33), channel_id=1, source_target_pairs={{0,15},{1,0},{2,1},{3,2},{4,3},{5,4},{6,5},{7,6},{8,7},{9,8},{10,9... | collective-permute-start | bytes 221192 | tf_op jit(solution)/shard_map/ppermute | solution.py:281
  51.1 31.7 %collective-permute-start.3 = (bf16[1,72,512]{2,1,0:T(8,128)(2,1)}, bf16[1,72,512]{2,1,0:T(8,128)(2,1)S(1)}, u32[]{:S(2)}, u32[]{:S(2)}) collective-permute-start(bf16[1,72,512]{2,1,0:T(8,128)(2,1)} %copy-done.8), channel_id=1, source_target_pairs={{0,255},{1,240},{2,241},{3,242},{4,243},{5,244},{6,245},{7,246},{8... | collective-permute-start | bytes 221192 | tf_op jit(solution)/shard_map/ppermute | solution.py:281
  56.2 26.6 %collective-permute-start.1 = (bf16[3,72,512]{2,1,0:T(8,128)(2,1)}, bf16[3,72,512]{2,1,0:T(8,128)(2,1)S(1)}, u32[]{:S(2)}, u32[]{:S(2)}) collective-permute-start(bf16[3,72,512]{2,1,0:T(8,128)(2,1)} %copy-done.7), channel_id=1, source_target_pairs={{0,240},{1,241},{2,242},{3,243},{4,244},{5,245},{6,246},{7,247},{8... | collective-permute-start | bytes 663560 | tf_op jit(solution)/shard_map/ppermute | solution.py:281
  56.5 26.4 %collective-permute-start = (bf16[4,72,512]{2,1,0:T(8,128)(2,1)S(1)}, bf16[4,72,512]{2,1,0:T(8,128)(2,1)S(1)}, u32[]{:S(2)}, u32[]{:S(2)}) collective-permute-start(bf16[4,72,512]{2,1,0:T(8,128)(2,1)S(1)} %get-tuple-element.30), channel_id=1, source_target_pairs={{0,16},{1,17},{2,18},{3,19},{4,20},{5,21},{6,22},{7,23},{8,24},{9,... | collective-permute-start | bytes 884744 | tf_op jit(solution)/shard_map/ppermute | solution.py:281
  57.7 2.2 %copy-start = (bf16[2048,1024]{1,0:T(8,128)(2,1)S(1)}, bf16[2048,1024]{1,0:T(8,128)(2,1)}, u32[]{:S(2)}) copy-start(bf16[2048,1024]{1,0:T(8,128)(2,1)} %merge_ref.3) | copy-start | bytes 12582916
  59.9 1.2 %copy-start.6 = (bf16[2,512,512]{2,1,0:T(8,128)(2,1)S(1)}, bf16[2,512,512]{2,1,0:T(8,128)(2,1)}, u32[]{:S(2)}) copy-start(bf16[2,512,512]{2,1,0:T(8,128)(2,1)} %wout_ref.7) | copy-start | bytes 3145732
  61.1 1.0 copy-start.12
  62.1 0.9 copy-start.16
  63.0 19.8 %copy-start.1 = (bf16[2048,1024]{1,0:T(8,128)(2,1)S(1)}, bf16[2048,1024]{1,0:T(8,128)(2,1)}, u32[]{:S(2)}) copy-start(bf16[2048,1024]{1,0:T(8,128)(2,1)} %merge_ref.3) | copy-start | bytes 12582916
  63.0 19.8 %copy-start.10 = (bf16[4,72,512]{2,1,0:T(8,128)(2,1)S(1)}, bf16[4,72,512]{2,1,0:T(8,128)(2,1)}, u32[]{:S(2)}) copy-start(bf16[4,72,512]{2,1,0:T(8,128)(2,1)} %copy-done.9) | copy-start | bytes 884740
  63.0 19.8 %copy-start.14 = (bf16[3,72,512]{2,1,0:T(8,128)(2,1)S(1)}, bf16[3,72,512]{2,1,0:T(8,128)(2,1)}, u32[]{:S(2)}) copy-start(bf16[3,72,512]{2,1,0:T(8,128)(2,1)} %copy-done.13) | copy-start | bytes 663556
  78.2 22.2 %collective-permute-start.14 = (bf16[1,18,1024]{2,1,0:T(8,128)(2,1)S(1)}, bf16[1,18,1024]{2,1,0:T(8,128)(2,1)S(1)}, u32[]{:S(2)}, u32[]{:S(2)}) collective-permute-start(bf16[1,18,1024]{2,1,0:T(8,128)(2,1)S(1)} %get-tuple-element.51), channel_id=1, source_target_pairs={{0,17},{1,18},{2,19},{3,20},{4,21},{5,22},{6,23},{7,24},{8,25},{9,... | collective-permute-start | bytes 110600 | tf_op jit(solution)/shard_map/ppermute | solution.py:281
  78.4 38.5 %collective-permute-start.12 = (bf16[4,18,1024]{2,1,0:T(8,128)(2,1)S(1)}, bf16[4,18,1024]{2,1,0:T(8,128)(2,1)S(1)}, u32[]{:S(2)}, u32[]{:S(2)}) collective-permute-start(bf16[4,18,1024]{2,1,0:T(8,128)(2,1)S(1)} %get-tuple-element.49), channel_id=1, source_target_pairs={{0,240},{1,241},{2,242},{3,243},{4,244},{5,245},{6,246},{7,247},{8... | collective-permute-start | bytes 442376 | tf_op jit(solution)/shard_map/ppermute | solution.py:281
  97.3 19.6 %collective-permute-start.4 = (bf16[4,18,1024]{2,1,0:T(8,128)(2,1)S(1)}, bf16[4,18,1024]{2,1,0:T(8,128)(2,1)S(1)}, u32[]{:S(2)}, u32[]{:S(2)}) collective-permute-start(bf16[4,18,1024]{2,1,0:T(8,128)(2,1)S(1)} %get-tuple-element.37), channel_id=1, source_target_pairs={{0,240},{1,241},{2,242},{3,243},{4,244},{5,245},{6,246},{7,247},{8... | collective-permute-start | bytes 442376 | tf_op jit(solution)/shard_map/ppermute | solution.py:281
  99.2 1.3 %collective-permute-start.15 = (bf16[1,18,1024]{2,1,0:T(8,128)(2,1)S(1)}, bf16[1,18,1024]{2,1,0:T(8,128)(2,1)S(1)}, u32[]{:S(2)}, u32[]{:S(2)}) collective-permute-start(bf16[1,18,1024]{2,1,0:T(8,128)(2,1)S(1)} %get-tuple-element.52), channel_id=1, source_target_pairs={{0,1},{1,2},{2,3},{3,4},{4,5},{5,6},{6,7},{7,8},{8,9},{9,10},{10,1... | collective-permute-start | bytes 110600 | tf_op jit(solution)/shard_map/ppermute | solution.py:281
  99.3 17.6 %collective-permute-start.13 = (bf16[3,18,1024]{2,1,0:T(8,128)(2,1)S(1)}, bf16[3,18,1024]{2,1,0:T(8,128)(2,1)S(1)}, u32[]{:S(2)}, u32[]{:S(2)}) collective-permute-start(bf16[3,18,1024]{2,1,0:T(8,128)(2,1)S(1)} %get-tuple-element.50), channel_id=1, source_target_pairs={{0,16},{1,17},{2,18},{3,19},{4,20},{5,21},{6,22},{7,23},{8,24},{9,... | collective-permute-start | bytes 331784 | tf_op jit(solution)/shard_map/ppermute | solution.py:281
  100.5 16.4 %collective-permute-start.5 = (bf16[3,18,1024]{2,1,0:T(8,128)(2,1)S(1)}, bf16[3,18,1024]{2,1,0:T(8,128)(2,1)S(1)}, u32[]{:S(2)}, u32[]{:S(2)}) collective-permute-start(bf16[3,18,1024]{2,1,0:T(8,128)(2,1)S(1)} %get-tuple-element.38), channel_id=1, source_target_pairs={{0,16},{1,17},{2,18},{3,19},{4,20},{5,21},{6,22},{7,23},{8,24},{9,... | collective-permute-start | bytes 331784 | tf_op jit(solution)/shard_map/ppermute | solution.py:281
  100.5 12.2 %collective-permute-start.6 = (bf16[1,18,1024]{2,1,0:T(8,128)(2,1)S(1)}, bf16[1,18,1024]{2,1,0:T(8,128)(2,1)S(1)}, u32[]{:S(2)}, u32[]{:S(2)}) collective-permute-start(bf16[1,18,1024]{2,1,0:T(8,128)(2,1)S(1)} %get-tuple-element.39), channel_id=1, source_target_pairs={{0,17},{1,18},{2,19},{3,20},{4,21},{5,22},{6,23},{7,24},{8,25},{9,... | collective-permute-start | bytes 110600 | tf_op jit(solution)/shard_map/ppermute | solution.py:281
  112.7 4.2 %collective-permute-start.7 = (bf16[1,18,1024]{2,1,0:T(8,128)(2,1)S(1)}, bf16[1,18,1024]{2,1,0:T(8,128)(2,1)S(1)}, u32[]{:S(2)}, u32[]{:S(2)}) collective-permute-start(bf16[1,18,1024]{2,1,0:T(8,128)(2,1)S(1)} %get-tuple-element.40), channel_id=1, source_target_pairs={{0,1},{1,2},{2,3},{3,4},{4,5},{5,6},{6,7},{7,8},{8,9},{9,10},{10,1... | collective-permute-start | bytes 110600 | tf_op jit(solution)/shard_map/ppermute | solution.py:281
  (1 other events, 0.6 us)

commit v2 on v1

v2 whole, which is shorter than its diff:
```python
import functools
import math

import jax
import jax.numpy as jnp
from jax import lax
from jax.experimental import pallas as pl
from jax.experimental.pallas import tpu as pltpu
from jax.sharding import PartitionSpec as P

HEADS = 16
WIN = 12
HALF = 6
QUAD = 72
SPAN = 4 * QUAD
WIDTH = 512
HEAD = WIDTH // HEADS
GROUP = 8
MAIN = 256
REST = SPAN - MAIN
SUB = 18
WINDOWS = 4
FAR = -1e30
SCALE = math.log2(math.e) / math.sqrt(HEAD)
NT = (((1,), (1,)), ((), ()))


def dot(a, b):
    return jnp.dot(a, b, preferred_element_type=jnp.float32)


def dot_nt(a, b):
    return lax.dot_general(a, b, NT, preferred_element_type=jnp.float32)


def normalized(values, eps):
    centered = values - jnp.mean(values, axis=-1, keepdims=True)
    return centered * lax.rsqrt(jnp.mean(centered * centered, axis=-1, keepdims=True) + eps)


def softened(scores, apart, straddles):
    half = SPAN // 2
    top, bottom = scores[:half], scores[half:]
    if apart is None:
        most = jnp.maximum(jnp.max(top, axis=0, keepdims=True), jnp.max(bottom, axis=0, keepdims=True))
        return jnp.exp2(scores - most).astype(jnp.bfloat16)
    if straddles:
        lane = lax.broadcasted_iota(jnp.int32, (1, MAIN), 1)
        from_top = jnp.where(lane < half, 0.0, apart)
        from_bottom = jnp.where(lane < half, apart, 0.0)
    else:
        from_top = jnp.full((1, MAIN), apart, jnp.float32)
        from_bottom = jnp.zeros((1, MAIN), jnp.float32)
    most = jnp.maximum(
        jnp.max(top, axis=0, keepdims=True) + from_top, jnp.max(bottom, axis=0, keepdims=True) + from_bottom
    )
    return jnp.concatenate(
        [
            jnp.exp2(top - (most - from_top)).astype(jnp.bfloat16),
            jnp.exp2(bottom - (most - from_bottom)).astype(jnp.bfloat16),
        ],
        axis=0,
    )


def attend_windows(fill, grid_ref, wqkv_ref, wout_ref, mod_ref, scratch, copies, apart):
    hidden_ref, query_ref, keys_ref, vt_ref, scores_ref, rest_ref, att_ref = scratch
    copy_qkv, copy_out = copies
    wide = GROUP * HEAD
    lane_head = lax.broadcasted_iota(jnp.int32, (1, wide), 1) // HEAD
    same = (
        lax.broadcasted_iota(jnp.int32, (wide, wide), 0) // HEAD
        == lax.broadcasted_iota(jnp.int32, (wide, wide), 1) // HEAD
    )
    fold = (
        lax.broadcasted_iota(jnp.int32, (REST, wide), 0) == lax.broadcasted_iota(jnp.int32, (REST, wide), 1) % HEAD
    ).astype(jnp.bfloat16)
    ones = jnp.ones((16, SPAN), jnp.bfloat16)

    def main_rows(w):
        return pl.ds(pl.multiple_of(w * MAIN, MAIN), MAIN)

    def rest_rows(w):
        return pl.ds(pl.multiple_of(WINDOWS * MAIN + w * REST, REST), REST)

    @pl.loop(0, WINDOWS)
    def _(w):
        fill(w)
        hidden = (normalized(grid_ref[w], 1e-06) * (1.0 + mod_ref[0:1]) + mod_ref[1:2]).astype(jnp.bfloat16)
        hidden_ref[main_rows(w)] = hidden[:MAIN]
        hidden_ref[rest_rows(w)] = hidden[MAIN:]

    copy_qkv.wait()
    query_ref[...] = (dot(hidden_ref[...], wqkv_ref[:, :WIDTH]) * SCALE).astype(jnp.bfloat16)
    keys_ref[...] = dot(hidden_ref[...], wqkv_ref[:, WIDTH : 2 * WIDTH]).astype(jnp.bfloat16)
    values = dot_nt(wqkv_ref[:, 2 * WIDTH :].T, hidden_ref[...]).astype(jnp.bfloat16)
    for w in range(WINDOWS):
        vt_ref[w, :, :MAIN] = values[:, w * MAIN : (w + 1) * MAIN]
        vt_ref[w, :, MAIN:] = values[:, WINDOWS * MAIN + w * REST : WINDOWS * MAIN + (w + 1) * REST]

    @pl.loop(0, WINDOWS)
    def _(w):
        for group in range(HEADS // GROUP):
            cols = slice(group * wide, (group + 1) * wide)
            kg = jnp.concatenate([keys_ref[main_rows(w), cols], keys_ref[rest_rows(w), cols]], axis=0)
            qm, qr = query_ref[main_rows(w), cols], query_ref[rest_rows(w), cols]
            for part in range(2):
                items = range(part * GROUP // 2, (part + 1) * GROUP // 2)
                masked = jnp.concatenate([kg * (lane_head == item).astype(jnp.bfloat16) for item in items], axis=0)
                scores_ref[2 * group + part] = dot_nt(masked, qm)
            rest_ref[group] = dot_nt(kg, jnp.concatenate([qr] * GROUP, axis=0) * same.astype(jnp.bfloat16))
        rest = []
        for group in range(HEADS // GROUP):
            cols = slice(group * wide, (group + 1) * wide)
            for item in range(GROUP):
                heads = slice((group * GROUP + item) * HEAD, (group * GROUP + item + 1) * HEAD)
                start = item % (GROUP // 2) * SPAN
                scores = scores_ref[2 * group + item // (GROUP // 2), start : start + SPAN]
                weights = softened(scores, apart, True)
                mixed = dot(jnp.concatenate([vt_ref[w, heads], ones], axis=0), weights)
                att_ref[heads] = mixed[:HEAD] * (1.0 / mixed[HEAD : HEAD + 1])
            weights = softened(rest_ref[group], apart, False)
            mixed = dot(jnp.concatenate([vt_ref[w, cols], ones], axis=0), weights)
            mixed = jnp.where(same, mixed[:wide] * (1.0 / mixed[wide : wide + 1]), 0.0).astype(jnp.bfloat16)
            rest.append(dot_nt(fold, mixed).astype(jnp.bfloat16))
        hidden_ref[main_rows(w)] = att_ref[...].T.astype(jnp.bfloat16)
        hidden_ref[rest_rows(w)] = jnp.concatenate(rest, axis=1)

    copy_out.wait()
    added = (1.0 + mod_ref[2:3]) * dot(hidden_ref[...], wout_ref[...])
    for w in range(WINDOWS):
        grid_ref[w, :MAIN] += added[w * MAIN : (w + 1) * MAIN]
        grid_ref[w, MAIN:] += added[WINDOWS * MAIN + w * REST : WINDOWS * MAIN + (w + 1) * REST]


def staged(layer, wqkv_hbm, wout_hbm, wqkv_ref, wout_ref, sems):
    copies = (
        pltpu.make_async_copy(wqkv_hbm.at[layer], wqkv_ref, sems.at[0]),
        pltpu.make_async_copy(wout_hbm.at[layer], wout_ref, sems.at[1]),
    )
    for copy in copies:
        copy.start()
    return copies


def first_kernel(
    pair, tokens_hbm, wqkv_hbm, wout_hbm, mod_ref, moving_hbm, staying_hbm, west_hbm, corner_hbm,
    grid_ref, *scratch,
):
    *scratch, wqkv_ref, wout_ref, sems, tokens_ref, pieces_ref, token_sems, piece_sems = scratch

    def brought(w):
        columns = pl.ds(w * WIN, WIN)
        return pltpu.make_async_copy(tokens_hbm.at[:, columns], tokens_ref.at[w], token_sems.at[w])

    for w in range(WINDOWS):
        brought(w).start()
    copies = staged(0, wqkv_hbm, wout_hbm, wqkv_ref, wout_ref, sems)

    def fill(w):
        brought(w).wait()
        for quad in range(4):
            for sub in range(4):
                for place in range(9):
                    i = quad // 2 * HALF + place // 3 * 2 + sub % 2
                    j = quad % 2 * HALF + place % 3 * 2 + sub // 2
                    row = quad * QUAD + sub * SUB + place * 2
                    grid_ref[w, row : row + 2] = tokens_ref[w, i, j, 2 * pair : 2 * pair + 2].astype(jnp.float32)

    attend_windows(fill, grid_ref, wqkv_ref, wout_ref, mod_ref.at[0], scratch, copies, None)
    for block in range(8):
        w, side = divmod(block, 2)
        for half in range(2):
            quad = 2 * half + side
            pieces_ref[half, block] = grid_ref[w, quad * QUAD : (quad + 1) * QUAD].astype(jnp.bfloat16)
    out = pieces_ref.at[pair], pieces_ref.at[1 - pair]
    ends = [
        pltpu.make_async_copy(source, target, piece_sems.at[index])
        for index, (source, target) in enumerate(
            [
                (out[0].at[pl.ds(1, 7)], moving_hbm),
                (out[1].at[pl.ds(1, 7)], staying_hbm),
                (out[1].at[pl.ds(0, 1)], west_hbm),
                (out[0].at[pl.ds(0, 1)], corner_hbm),
            ]
        )
    ]
    for end in ends:
        end.start()
    for end in ends:
        end.wait()


def second_kernel(
    pair, apart_ref, staying_hbm, received_hbm, east_hbm, corner_hbm, wqkv_hbm, wout_hbm, mod_ref, merge_hbm,
    away_ref, own_ref, back_east_ref, back_corner_ref,
    grid_ref, *scratch,
):
    *scratch, wqkv_ref, wout_ref, sems, merge_ref, pieces_ref, joined_ref, merge_sem, piece_sems = scratch
    kept, got = pieces_ref.at[pair], pieces_ref.at[1 - pair]
    begins = [
        pltpu.make_async_copy(source, target, piece_sems.at[index])
        for index, (source, target) in enumerate(
            [
                (staying_hbm, kept.at[pl.ds(0, 7)]),
                (received_hbm, got.at[pl.ds(0, 7)]),
                (east_hbm, kept.at[pl.ds(7, 1)]),
                (corner_hbm, got.at[pl.ds(7, 1)]),
            ]
        )
    ]
    for begin in begins:
        begin.start()
    copies = staged(1, wqkv_hbm, wout_hbm, wqkv_ref, wout_ref, sems)
    copy_merge = pltpu.make_async_copy(merge_hbm, merge_ref, merge_sem)
    copy_merge.start()
    for begin in begins:
        begin.wait()

    def fill(w):
        for quad in range(4):
            grid_ref[w, quad * QUAD : (quad + 1) * QUAD] = pieces_ref[quad // 2, 2 * w + quad % 2].astype(jnp.float32)

    attend_windows(fill, grid_ref, wqkv_ref, wout_ref, mod_ref.at[1], scratch, copies, apart_ref[pair])

    @pl.loop(0, WINDOWS)
    def _(w):
        for quad in range(4):
            for sub in range(4):
                start = quad * QUAD + sub * SUB
                joined_ref[w, quad * SUB : (quad + 1) * SUB, sub * WIDTH : (sub + 1) * WIDTH] = (
                    grid_ref[w, start : start + SUB].astype(jnp.bfloat16).astype(jnp.float32)
                )

    flat = jnp.concatenate([normalized(joined_ref[w], 1e-05).astype(jnp.bfloat16) for w in range(WINDOWS)], axis=0)
    copy_merge.wait()
    merged = dot(flat, merge_ref[...])
    for block in range(8):
        w, side = divmod(block, 2)
        for half in range(2):
            start = w * QUAD + (2 * half + side) * SUB
            piece = merged[start : start + SUB].astype(jnp.bfloat16)
            if half == pair:
                target, last = own_ref, back_east_ref
            else:
                target, last = away_ref, back_corner_ref
            if block < 7:
                target[block] = piece
            else:
                last[0] = piece


def last_kernel(*refs):
    out_ref = refs[-1]
    for pair in range(2):
        own, back, from_west, corner = refs[4 * pair : 4 * pair + 4]
        for half in range(2):
            for block in range(8):
                if half != pair:
                    ref = own if block else from_west
                else:
                    ref = back if block else corner
                for place in range(9):
                    i, j = half * 3 + place // 3, block * 3 + place % 3
                    out_ref[i, j, 2 * pair : 2 * pair + 2] = ref[max(block - 1, 0), 2 * place : 2 * place + 2]


def whole(*shape):
    return pl.BlockSpec(shape, lambda: (0,) * len(shape))


def struct(*shape):
    return jax.ShapeDtypeStruct(shape, jnp.bfloat16)


LIMIT = 36 * 1024 * 1024
HBM = pl.BlockSpec(memory_space=pltpu.HBM)
LAYER_SCRATCH = [
    pltpu.VMEM((WINDOWS, SPAN, WIDTH), jnp.float32),
    pltpu.VMEM((WINDOWS * SPAN, WIDTH), jnp.bfloat16),
    pltpu.VMEM((WINDOWS * SPAN, WIDTH), jnp.bfloat16),
    pltpu.VMEM((WINDOWS * SPAN, WIDTH), jnp.bfloat16),
    pltpu.VMEM((WINDOWS, WIDTH, SPAN), jnp.bfloat16),
    pltpu.VMEM((4, HEADS // 4 * SPAN, MAIN), jnp.float32),
    pltpu.VMEM((HEADS // GROUP, SPAN, MAIN), jnp.float32),
    pltpu.VMEM((WIDTH, MAIN), jnp.float32),
    pltpu.VMEM((WIDTH, 3 * WIDTH), jnp.bfloat16),
    pltpu.VMEM((WIDTH, WIDTH), jnp.bfloat16),
    pltpu.SemaphoreType.DMA((2,)),
]
LAYER_SPECS = [HBM, HBM, whole(2, 3, WIDTH)]
LAYER_FLOPS = 2 * 4 * SPAN * (4 * WIDTH * WIDTH + 2 * 8 * SPAN * WIDTH)
COUNTS = (7, 7, 1, 1)


def first_layer(pair, tokens, layers):
    return pl.pallas_call(
        functools.partial(first_kernel, pair),
        in_specs=[HBM] + LAYER_SPECS,
        out_specs=[HBM] * 4,
        out_shape=[struct(n, QUAD, WIDTH) for n in COUNTS],
        scratch_shapes=LAYER_SCRATCH
        + [
            pltpu.VMEM((WINDOWS, WIN, WIN, 4, WIDTH), jnp.bfloat16),
            pltpu.VMEM((2, 8, QUAD, WIDTH), jnp.bfloat16),
            pltpu.SemaphoreType.DMA((WINDOWS,)),
            pltpu.SemaphoreType.DMA((4,)),
        ],
        compiler_params=pltpu.CompilerParams(vmem_limit_bytes=LIMIT),
        cost_estimate=pl.CostEstimate(flops=LAYER_FLOPS, bytes_accessed=5 << 20, transcendentals=16 * 4 * SPAN * SPAN),
        name=f"layer0_pair{pair}",
    )(tokens, *layers)


def second_layer(pair, apart, pieces, layers, w_merge):
    return pl.pallas_call(
        functools.partial(second_kernel, pair),
        in_specs=[pl.BlockSpec(memory_space=pltpu.SMEM)] + [HBM] * 4 + LAYER_SPECS + [HBM],
        out_specs=[whole(n, SUB, 2 * WIDTH) for n in COUNTS],
        out_shape=[struct(n, SUB, 2 * WIDTH) for n in COUNTS],
        scratch_shapes=LAYER_SCRATCH
        + [
            pltpu.VMEM((4 * WIDTH, 2 * WIDTH), jnp.bfloat16),
            pltpu.VMEM((2, 8, QUAD, WIDTH), jnp.bfloat16),
            pltpu.VMEM((4, QUAD, 4 * WIDTH), jnp.float32),
            pltpu.SemaphoreType.DMA(()),
            pltpu.SemaphoreType.DMA((4,)),
        ],
        compiler_params=pltpu.CompilerParams(vmem_limit_bytes=LIMIT),
        cost_estimate=pl.CostEstimate(
            flops=LAYER_FLOPS + 2 * SPAN * 8 * WIDTH * WIDTH, bytes_accessed=8 << 20, transcendentals=16 * 4 * SPAN * SPAN
        ),
        name=f"layer1_pair{pair}",
    )(apart, *pieces, *layers, w_merge)


def moved(value, down, east):
    lats, lons = lax.axis_size("lat"), lax.axis_size("lon")
    pairs = [
        (lat * lons + lon, (lat + down) % lats * lons + (lon + east) % lons) for lat in range(lats) for lon in range(lons)
    ]
    return lax.ppermute(value, ("lat", "lon"), pairs)


def body(tokens, w_qkv, w_out, modulation, w_merge):
    layers = (w_qkv, w_out, modulation)
    lat, last = lax.axis_index("lat"), lax.axis_size("lat") - 1
    apart = jnp.where(jnp.stack([lat == last, lat == 0]), FAR, 0.0).astype(jnp.float32)
    firsts = [first_layer(pair, tokens, layers) for pair in range(2)]
    seconds = []
    for pair, (moving, staying, west, corner) in enumerate(firsts):
        way = 2 * pair - 1
        pieces = (staying, moved(moving, way, 0), moved(west, 0, -1), moved(corner, way, -1))
        seconds.append(second_layer(pair, apart, pieces, layers, w_merge))
    placed = []
    for pair, (away, own, east, corner) in enumerate(seconds):
        way = 1 - 2 * pair
        placed += [own, moved(away, way, 0), moved(east, 0, 1), moved(corner, way, 1)]
    rows, cols = tokens.shape[0] // 2, tokens.shape[1] // 2
    return pl.pallas_call(
        last_kernel,
        out_shape=struct(rows, cols, 4, 2 * WIDTH),
        compiler_params=pltpu.CompilerParams(vmem_limit_bytes=LIMIT),
        name="placing",
    )(*placed)


def solution(mesh):
    in_specs = (P("lat", "lon", None, None), P(), P(), P(), P())
    out_specs = P("lat", "lon", None, None)
    return jax.shard_map(body, mesh=mesh, in_specs=in_specs, out_specs=out_specs, check_vma=False)
```

time: 121 us -> 107 us (0.88); the launches traced: 119 us -> 106 us
  starting transfers between devices: 31.7 us -> 22.9 us
  waiting for transfers between devices: 13.2 us -> 8.21 us
  Pallas kernels: 58.6 us -> 62.7 us
  local copies, waits for them, and re-layouts: 14.9 us -> 12.3 us
    ppermute x16 -> x12, starting transfers between devices: 31.7 us -> 22.9 us  [moved(): return lax.ppermute(value, ('lat', 'lon'), pairs)]
    ppermute x16 -> x12, waiting for transfers between devices: 13.2 us -> 8.21 us  [moved(): return lax.ppermute(value, ('lat', 'lon'), pairs)]
    pallas_call x4, Pallas kernels: 56.9 us -> 61 us  [the longest x2 32.3 us: second_layer(): pl.pallas_call(functools.partial(second_kernel, pair), in_specs=[pl.Block...]
    unnamed x35 -> x25, local copies, waits for them, and re-layouts: 14.9 us -> 12.3 us
  transfers between devices with their start and end apart: 16 -> 12, of which waited for: 2 -> 3; matrix products, arithmetic and copies ran while one was open for 0% -> 0% of each run, Pallas kernels for 36% -> 44%
where the time goes in v2:
time: 107 us; the launch traced here: 106 us
  Pallas kernels  62.7 us (59%)
  starting transfers between devices  22.9 us (21%)
  local copies, waits for them, and re-layouts  12.3 us (11%)
  waiting for transfers between devices  8.21 us (8%)
    pallas_call x2, Pallas kernels, second_layer(): pl.pallas_call(functools.partial(second_kernel, pair), in_specs=[pl.Block...  32.3 us
    pallas_call x2, Pallas kernels, first_layer(): pl.pallas_call(functools.partial(first_kernel, pair), in_specs=[HBM] + LA...  28.7 us
    ppermute x12, starting transfers between devices, moved(): return lax.ppermute(value, ('lat', 'lon'), pairs)  22.9 us
    unnamed x25, local copies, waits for them, and re-layouts  12.3 us
    ppermute x12, waiting for transfers between devices, moved(): return lax.ppermute(value, ('lat', 'lon'), pairs)  8.21 us
  transfers between devices with their start and end apart: 12, of which 3 were waited for; matrix products, arithmetic and copies ran while one was open for 0% of the time, Pallas kernels for 44%

profile of v2, /device:TPU:1, one launch (start us, length us, event | category | flops | bytes accessed | tf_op | source)
XLA Modules:
  0.0 106.3 jit_solution(16965306345454589603)
XLA Ops:
  0.0 0.7 copy.6.mod_ref
  0.7 1.9 %copy-done.2 = bf16[2,512,1536]{2,1,0:T(8,128)(2,1)S(1)} copy-done((bf16[2,512,1536]{2,1,0:T(8,128)(2,1)S(1)}, bf16[2,512,1536]{2,1,0:T(8,128)(2,1)}, u32[]{:S(2)}) %copy-start.2) | copy-done | bytes 3145752
  2.6 1.7 %copy-done.4 = bf16[12,48,4,512]{3,2,1,0:T(4,128)(2,1)S(1)} copy-done((bf16[12,48,4,512]{3,2,1,0:T(4,128)(2,1)S(1)}, bf16[12,48,4,512]{3,2,1,0:T(4,128)(2,1)}, u32[]{:S(2)}) %copy-start.4) | copy-done | bytes 2359320
  4.3 1.2 %copy-done.5 = bf16[2,512,512]{2,1,0:T(8,128)(2,1)S(1)} copy-done((bf16[2,512,512]{2,1,0:T(8,128)(2,1)S(1)}, bf16[2,512,512]{2,1,0:T(8,128)(2,1)}, u32[]{:S(2)}) %copy-start.5) | copy-done | bytes 1048600
  5.5 14.4 %layer0_pair1.1 = (bf16[7,72,512]{2,1,0:T(8,128)(2,1)}, bf16[7,72,512]{2,1,0:T(8,128)(2,1)S(1)}, bf16[1,72,512]{2,1,0:T(8,128)(2,1)}, bf16[1,72,512]{2,1,0:T(8,128)(2,1)}) custom-call(bf16[12,48,4,512]{3,2,1,0:T(4,128)(2,1)S(1)} %copy-done.4, bf16[2,512,1536]{2,1,0:T(8,128)(2,1)S(1)} %copy-done.2, bf16[2,512,512]{2,1,0:T(8,128)(2,1)S(1)} %copy-done.5, ...), custom_call_target="tpu_custom_call" | custom-call | flops 7851737088 | bytes 5242880 | tf_op jit(solution)/shard_map/layer0_pair1/pallas_call | solution.py:297
  19.9 0.8 copy-done.10
  20.7 3.3 %collective-permute-start.7 = (bf16[1,72,512]{2,1,0:T(8,128)(2,1)}, bf16[1,72,512]{2,1,0:T(8,128)(2,1)S(1)}, u32[]{:S(2)}, u32[]{:S(2)}) collective-permute-start(bf16[1,72,512]{2,1,0:T(8,128)(2,1)} %get-tuple-element.31), channel_id=1, source_target_pairs={{0,15},{1,0},{2,1},{3,2},{4,3},{5,4},{6,5},{7,6},{8,7},{9,8},{10,9... | collective-permute-start | bytes 221192 | tf_op jit(solution)/shard_map/ppermute | solution.py:342
  23.9 3.0 %collective-permute-start.8 = (bf16[1,72,512]{2,1,0:T(8,128)(2,1)}, bf16[1,72,512]{2,1,0:T(8,128)(2,1)}, u32[]{:S(2)}, u32[]{:S(2)}) collective-permute-start(bf16[1,72,512]{2,1,0:T(8,128)(2,1)} %get-tuple-element.32), channel_id=1, source_target_pairs={{0,31},{1,16},{2,17},{3,18},{4,19},{5,20},{6,21},{7,22},{8,23},{9,... | collective-permute-start | bytes 221192 | tf_op jit(solution)/shard_map/ppermute | solution.py:342
  26.9 1.6 %collective-permute-start.6 = (bf16[7,72,512]{2,1,0:T(8,128)(2,1)}, bf16[7,72,512]{2,1,0:T(8,128)(2,1)}, u32[]{:S(2)}, u32[]{:S(2)}) collective-permute-start(bf16[7,72,512]{2,1,0:T(8,128)(2,1)} %get-tuple-element.30), channel_id=1, source_target_pairs={{0,16},{1,17},{2,18},{3,19},{4,20},{5,21},{6,22},{7,23},{8,24},{9,... | collective-permute-start | bytes 1548296 | tf_op jit(solution)/shard_map/ppermute | solution.py:342
  28.6 14.3 %layer0_pair0.1 = (bf16[7,72,512]{2,1,0:T(8,128)(2,1)S(1)}, bf16[7,72,512]{2,1,0:T(8,128)(2,1)S(1)}, bf16[1,72,512]{2,1,0:T(8,128)(2,1)S(1)}, bf16[1,72,512]{2,1,0:T(8,128)(2,1)S(1)}) custom-call(bf16[12,48,4,512]{3,2,1,0:T(4,128)(2,1)S(1)} %copy-done.4, bf16[2,512,1536]{2,1,0:T(8,128)(2,1)S(1)} %copy-done.2, bf16[2,512,512]{2,1,0:T(8,128)(2,1)S(1)} %copy-done.5, ...), custom_call_target="tpu_custom_call" | custom-call | flops 7851737088 | bytes 5242880 | tf_op jit(solution)/shard_map/layer0_pair0/pallas_call | solution.py:297
  42.9 0.8 copy-done.7
  43.7 0.8 copy-done.8
  44.5 0.8 collective-permute-start.1
  45.3 4.6 %collective-permute-start.2 = (bf16[1,72,512]{2,1,0:T(8,128)(2,1)S(1)}, bf16[1,72,512]{2,1,0:T(8,128)(2,1)S(1)}, u32[]{:S(2)}, u32[]{:S(2)}) collective-permute-start(bf16[1,72,512]{2,1,0:T(8,128)(2,1)S(1)} %get-tuple-element.24), channel_id=1, source_target_pairs={{0,255},{1,240},{2,241},{3,242},{4,243},{5,244},{6,245},{7,246},{8... | collective-permute-start | bytes 221192 | tf_op jit(solution)/shard_map/ppermute | solution.py:342
  49.8 0.1 add_select_fusion.apart_ref
  49.9 0.0 collective-permute-done.7.east_hbm
  49.9 1.5 %collective-permute-start = (bf16[7,72,512]{2,1,0:T(8,128)(2,1)}, bf16[7,72,512]{2,1,0:T(8,128)(2,1)S(1)}, u32[]{:S(2)}, u32[]{:S(2)}) collective-permute-start(bf16[7,72,512]{2,1,0:T(8,128)(2,1)} %copy-done.7), channel_id=1, source_target_pairs={{0,240},{1,241},{2,242},{3,243},{4,244},{5,245},{6,246},{7,247},{8... | collective-permute-start | bytes 1548296 | tf_op jit(solution)/shard_map/ppermute | solution.py:342
  51.4 0.0 collective-permute-done.8.corner_hbm
  51.5 0.0 copy-start
  51.5 2.2 %copy-done = bf16[2048,1024]{1,0:T(8,128)(2,1)S(1)} copy-done((bf16[2048,1024]{1,0:T(8,128)(2,1)S(1)}, bf16[2048,1024]{1,0:T(8,128)(2,1)}, u32[]{:S(2)}) %copy-start) | copy-done | bytes 4194328
  53.7 1.2 %copy-done.6 = bf16[2,512,512]{2,1,0:T(8,128)(2,1)S(1)} copy-done((bf16[2,512,512]{2,1,0:T(8,128)(2,1)S(1)}, bf16[2,512,512]{2,1,0:T(8,128)(2,1)}, u32[]{:S(2)}) %copy-start.6) | copy-done | bytes 1048600
  54.9 1.0 copy-done.11
  55.9 16.4 %layer1_pair1.1 = (bf16[7,18,1024]{2,1,0:T(8,128)(2,1)S(1)}, bf16[7,18,1024]{2,1,0:T(8,128)(2,1)S(1)}, bf16[1,18,1024]{2,1,0:T(8,128)(2,1)S(1)}, bf16[1,18,1024]{2,1,0:T(8,128)(2,1)S(1)}) custom-call(f32[2]{0:T(128)S(1)} %add_select_fusion.apart_ref, bf16[7,72,512]{2,1,0:T(8,128)(2,1)S(1)} %copy-done.11, ...), custom_call_target="tpu_custom_call" | custom-call | flops 9059696640 | bytes 8388608 | tf_op jit(solution)/shard_map/layer1_pair1/pallas_call | solution.py:316
  72.3 1.8 %collective-permute-start.9 = (bf16[7,18,1024]{2,1,0:T(8,128)(2,1)S(1)}, bf16[7,18,1024]{2,1,0:T(8,128)(2,1)S(1)}, u32[]{:S(2)}, u32[]{:S(2)}) collective-permute-start(bf16[7,18,1024]{2,1,0:T(8,128)(2,1)S(1)} %get-tuple-element.34), channel_id=1, source_target_pairs={{0,240},{1,241},{2,242},{3,243},{4,244},{5,245},{6,246},{7,247},{8... | collective-permute-start | bytes 774152 | tf_op jit(solution)/shard_map/ppermute | solution.py:342
  74.1 15.9 %layer1_pair0.1 = (bf16[7,18,1024]{2,1,0:T(8,128)(2,1)S(1)}, bf16[7,18,1024]{2,1,0:T(8,128)(2,1)S(1)}, bf16[1,18,1024]{2,1,0:T(8,128)(2,1)S(1)}, bf16[1,18,1024]{2,1,0:T(8,128)(2,1)S(1)}) custom-call(f32[2]{0:T(128)S(1)} %add_select_fusion.apart_ref, bf16[7,72,512]{2,1,0:T(8,128)(2,1)S(1)} %copy-done.9, ...), custom_call_target="tpu_custom_call" | custom-call | flops 9059696640 | bytes 8388608 | tf_op jit(solution)/shard_map/layer1_pair0/pallas_call | solution.py:316
  90.0 0.1 collective-permute-start.3
  90.1 1.6 %collective-permute-start.10 = (bf16[1,18,1024]{2,1,0:T(8,128)(2,1)S(1)}, bf16[1,18,1024]{2,1,0:T(8,128)(2,1)S(1)}, u32[]{:S(2)}, u32[]{:S(2)}) collective-permute-start(bf16[1,18,1024]{2,1,0:T(8,128)(2,1)S(1)} %get-tuple-element.35), channel_id=1, source_target_pairs={{0,1},{1,2},{2,3},{3,4},{4,5},{5,6},{6,7},{7,8},{8,9},{9,10},{10,1... | collective-permute-start | bytes 110600 | tf_op jit(solution)/shard_map/ppermute | solution.py:342
  91.7 4.7 %collective-permute-start.11 = (bf16[1,18,1024]{2,1,0:T(8,128)(2,1)S(1)}, bf16[1,18,1024]{2,1,0:T(8,128)(2,1)S(1)}, u32[]{:S(2)}, u32[]{:S(2)}) collective-permute-start(bf16[1,18,1024]{2,1,0:T(8,128)(2,1)S(1)} %get-tuple-element.36), channel_id=1, source_target_pairs={{0,241},{1,242},{2,243},{3,244},{4,245},{5,246},{6,247},{7,248},{8... | collective-permute-start | bytes 110600 | tf_op jit(solution)/shard_map/ppermute | solution.py:342
  96.4 1.2 %collective-permute-done.11.refs_7_ = bf16[1,18,1024]{2,1,0:T(8,128)(2,1)S(1)} collective-permute-done((bf16[1,18,1024]{2,1,0:T(8,128)(2,1)S(1)}, bf16[1,18,1024]{2,1,0:T(8,128)(2,1)S(1)}, u32[]{:S(2)}, u32[]{:S(2)}) %collective-permute-start.11) | collective-permute-done | bytes 36896 | tf_op jit(solution)/shard_map/ppermute | solution.py:342
  97.6 2.8 %collective-permute-done.4.refs_2_ = bf16[1,18,1024]{2,1,0:T(8,128)(2,1)S(1)} collective-permute-done((bf16[1,18,1024]{2,1,0:T(8,128)(2,1)S(1)}, bf16[1,18,1024]{2,1,0:T(8,128)(2,1)S(1)}, u32[]{:S(2)}, u32[]{:S(2)}) %collective-permute-start.4) | collective-permute-done | bytes 36896 | tf_op jit(solution)/shard_map/ppermute | solution.py:342
  100.3 4.3 %collective-permute-done.5.refs_3_ = bf16[1,18,1024]{2,1,0:T(8,128)(2,1)S(1)} collective-permute-done((bf16[1,18,1024]{2,1,0:T(8,128)(2,1)S(1)}, bf16[1,18,1024]{2,1,0:T(8,128)(2,1)S(1)}, u32[]{:S(2)}, u32[]{:S(2)}) %collective-permute-start.5) | collective-permute-done | bytes 36896 | tf_op jit(solution)/shard_map/ppermute | solution.py:342
  104.6 1.7 %placing.1 = bf16[6,24,4,1024]{3,2,1,0:T(4,128)(2,1)} custom-call(bf16[7,18,1024]{2,1,0:T(8,128)(2,1)S(1)} %get-tuple-element.25.refs_0_, bf16[7,18,1024]{2,1,0:T(8,128)(2,1)S(1)} %collective-permute-done.3.refs_1_, bf16[1,18,1024]{2,1,0:T(8,128)(2,1)S(1)} %collective-permute-done.4.refs_2_, bf16[1,18,1024]{2,1,0:T(8,128)(2,1)S(1)} %collective-permute-done.5.refs_3_, ...), custom_call_target="tpu_custom_call" | custom-call | tf_op jit(solution)/shard_map/placing/pallas_call | solution.py:360
  (23 shorter events, 0.0 us)
Async XLA Ops:
  0.7 1.9 %copy-start.2 = (bf16[2,512,1536]{2,1,0:T(8,128)(2,1)S(1)}, bf16[2,512,1536]{2,1,0:T(8,128)(2,1)}, u32[]{:S(2)}) copy-start(bf16[2,512,1536]{2,1,0:T(8,128)(2,1)} %wqkv_hbm.7) | copy-start | bytes 9437188
  2.6 1.7 %copy-start.4 = (bf16[12,48,4,512]{3,2,1,0:T(4,128)(2,1)S(1)}, bf16[12,48,4,512]{3,2,1,0:T(4,128)(2,1)}, u32[]{:S(2)}) copy-start(bf16[12,48,4,512]{3,2,1,0:T(4,128)(2,1)} %tokens_hbm.3) | copy-start | bytes 7077892
  4.3 1.2 %copy-start.5 = (bf16[2,512,512]{2,1,0:T(8,128)(2,1)S(1)}, bf16[2,512,512]{2,1,0:T(8,128)(2,1)}, u32[]{:S(2)}) copy-start(bf16[2,512,512]{2,1,0:T(8,128)(2,1)} %wout_hbm.7) | copy-start | bytes 3145732
  19.9 0.8 copy-start.10
  20.7 29.2 %collective-permute-start.7 = (bf16[1,72,512]{2,1,0:T(8,128)(2,1)}, bf16[1,72,512]{2,1,0:T(8,128)(2,1)S(1)}, u32[]{:S(2)}, u32[]{:S(2)}) collective-permute-start(bf16[1,72,512]{2,1,0:T(8,128)(2,1)} %get-tuple-element.31), channel_id=1, source_target_pairs={{0,15},{1,0},{2,1},{3,2},{4,3},{5,4},{6,5},{7,6},{8,7},{9,8},{10,9... | collective-permute-start | bytes 221192 | tf_op jit(solution)/shard_map/ppermute | solution.py:342
  23.9 27.5 %collective-permute-start.8 = (bf16[1,72,512]{2,1,0:T(8,128)(2,1)}, bf16[1,72,512]{2,1,0:T(8,128)(2,1)}, u32[]{:S(2)}, u32[]{:S(2)}) collective-permute-start(bf16[1,72,512]{2,1,0:T(8,128)(2,1)} %get-tuple-element.32), channel_id=1, source_target_pairs={{0,31},{1,16},{2,17},{3,18},{4,19},{5,20},{6,21},{7,22},{8,23},{9,... | collective-permute-start | bytes 221192 | tf_op jit(solution)/shard_map/ppermute | solution.py:342
  26.9 24.5 %copy-start.3 = (bf16[2,512,1536]{2,1,0:T(8,128)(2,1)S(1)}, bf16[2,512,1536]{2,1,0:T(8,128)(2,1)}, u32[]{:S(2)}) copy-start(bf16[2,512,1536]{2,1,0:T(8,128)(2,1)} %wqkv_hbm.7) | copy-start | bytes 9437188
  26.9 24.5 %collective-permute-start.6 = (bf16[7,72,512]{2,1,0:T(8,128)(2,1)}, bf16[7,72,512]{2,1,0:T(8,128)(2,1)}, u32[]{:S(2)}, u32[]{:S(2)}) collective-permute-start(bf16[7,72,512]{2,1,0:T(8,128)(2,1)} %get-tuple-element.30), channel_id=1, source_target_pairs={{0,16},{1,17},{2,18},{3,19},{4,20},{5,21},{6,22},{7,23},{8,24},{9,... | collective-permute-start | bytes 1548296 | tf_op jit(solution)/shard_map/ppermute | solution.py:342
  42.9 0.8 copy-start.7
  43.7 0.8 copy-start.8
  44.5 29.6 %collective-permute-start.1 = (bf16[1,72,512]{2,1,0:T(8,128)(2,1)S(1)}, bf16[1,72,512]{2,1,0:T(8,128)(2,1)S(1)}, u32[]{:S(2)}, u32[]{:S(2)}) collective-permute-start(bf16[1,72,512]{2,1,0:T(8,128)(2,1)S(1)} %get-tuple-element.23), channel_id=1, source_target_pairs={{0,15},{1,0},{2,1},{3,2},{4,3},{5,4},{6,5},{7,6},{8,7},{9,8},{10,9... | collective-permute-start | bytes 221192 | tf_op jit(solution)/shard_map/ppermute | solution.py:342
  45.3 28.8 %collective-permute-start.2 = (bf16[1,72,512]{2,1,0:T(8,128)(2,1)S(1)}, bf16[1,72,512]{2,1,0:T(8,128)(2,1)S(1)}, u32[]{:S(2)}, u32[]{:S(2)}) collective-permute-start(bf16[1,72,512]{2,1,0:T(8,128)(2,1)S(1)} %get-tuple-element.24), channel_id=1, source_target_pairs={{0,255},{1,240},{2,241},{3,242},{4,243},{5,244},{6,245},{7,246},{8... | collective-permute-start | bytes 221192 | tf_op jit(solution)/shard_map/ppermute | solution.py:342
  49.9 24.2 %collective-permute-start = (bf16[7,72,512]{2,1,0:T(8,128)(2,1)}, bf16[7,72,512]{2,1,0:T(8,128)(2,1)S(1)}, u32[]{:S(2)}, u32[]{:S(2)}) collective-permute-start(bf16[7,72,512]{2,1,0:T(8,128)(2,1)} %copy-done.7), channel_id=1, source_target_pairs={{0,240},{1,241},{2,242},{3,243},{4,244},{5,245},{6,246},{7,247},{8... | collective-permute-start | bytes 1548296 | tf_op jit(solution)/shard_map/ppermute | solution.py:342
  51.5 2.2 %copy-start = (bf16[2048,1024]{1,0:T(8,128)(2,1)S(1)}, bf16[2048,1024]{1,0:T(8,128)(2,1)}, u32[]{:S(2)}) copy-start(bf16[2048,1024]{1,0:T(8,128)(2,1)} %merge_hbm.3) | copy-start | bytes 12582916
  53.7 1.2 %copy-start.6 = (bf16[2,512,512]{2,1,0:T(8,128)(2,1)S(1)}, bf16[2,512,512]{2,1,0:T(8,128)(2,1)}, u32[]{:S(2)}) copy-start(bf16[2,512,512]{2,1,0:T(8,128)(2,1)} %wout_hbm.7) | copy-start | bytes 3145732
  54.9 1.0 copy-start.11
  55.9 18.2 %copy-start.1 = (bf16[2048,1024]{1,0:T(8,128)(2,1)S(1)}, bf16[2048,1024]{1,0:T(8,128)(2,1)}, u32[]{:S(2)}) copy-start(bf16[2048,1024]{1,0:T(8,128)(2,1)} %merge_hbm.3) | copy-start | bytes 12582916
  55.9 18.2 %copy-start.9 = (bf16[7,72,512]{2,1,0:T(8,128)(2,1)S(1)}, bf16[7,72,512]{2,1,0:T(8,128)(2,1)}, u32[]{:S(2)}) copy-start(bf16[7,72,512]{2,1,0:T(8,128)(2,1)} %copy-done.8) | copy-start | bytes 1548292
  72.3 32.3 %collective-permute-start.9 = (bf16[7,18,1024]{2,1,0:T(8,128)(2,1)S(1)}, bf16[7,18,1024]{2,1,0:T(8,128)(2,1)S(1)}, u32[]{:S(2)}, u32[]{:S(2)}) collective-permute-start(bf16[7,18,1024]{2,1,0:T(8,128)(2,1)S(1)} %get-tuple-element.34), channel_id=1, source_target_pairs={{0,240},{1,241},{2,242},{3,243},{4,244},{5,245},{6,246},{7,247},{8... | collective-permute-start | bytes 774152 | tf_op jit(solution)/shard_map/ppermute | solution.py:342
  90.0 14.6 %collective-permute-start.3 = (bf16[7,18,1024]{2,1,0:T(8,128)(2,1)S(1)}, bf16[7,18,1024]{2,1,0:T(8,128)(2,1)S(1)}, u32[]{:S(2)}, u32[]{:S(2)}) collective-permute-start(bf16[7,18,1024]{2,1,0:T(8,128)(2,1)S(1)} %get-tuple-element.26), channel_id=1, source_target_pairs={{0,16},{1,17},{2,18},{3,19},{4,20},{5,21},{6,22},{7,23},{8,24},{9,... | collective-permute-start | bytes 774152 | tf_op jit(solution)/shard_map/ppermute | solution.py:342
  90.1 6.3 %collective-permute-start.10 = (bf16[1,18,1024]{2,1,0:T(8,128)(2,1)S(1)}, bf16[1,18,1024]{2,1,0:T(8,128)(2,1)S(1)}, u32[]{:S(2)}, u32[]{:S(2)}) collective-permute-start(bf16[1,18,1024]{2,1,0:T(8,128)(2,1)S(1)} %get-tuple-element.35), channel_id=1, source_target_pairs={{0,1},{1,2},{2,3},{3,4},{4,5},{5,6},{6,7},{7,8},{8,9},{9,10},{10,1... | collective-permute-start | bytes 110600 | tf_op jit(solution)/shard_map/ppermute | solution.py:342
  91.7 5.9 %collective-permute-start.11 = (bf16[1,18,1024]{2,1,0:T(8,128)(2,1)S(1)}, bf16[1,18,1024]{2,1,0:T(8,128)(2,1)S(1)}, u32[]{:S(2)}, u32[]{:S(2)}) collective-permute-start(bf16[1,18,1024]{2,1,0:T(8,128)(2,1)S(1)} %get-tuple-element.36), channel_id=1, source_target_pairs={{0,241},{1,242},{2,243},{3,244},{4,245},{5,246},{6,247},{7,248},{8... | collective-permute-start | bytes 110600 | tf_op jit(solution)/shard_map/ppermute | solution.py:342
  96.4 3.9 %collective-permute-start.4 = (bf16[1,18,1024]{2,1,0:T(8,128)(2,1)S(1)}, bf16[1,18,1024]{2,1,0:T(8,128)(2,1)S(1)}, u32[]{:S(2)}, u32[]{:S(2)}) collective-permute-start(bf16[1,18,1024]{2,1,0:T(8,128)(2,1)S(1)} %get-tuple-element.27), channel_id=1, source_target_pairs={{0,1},{1,2},{2,3},{3,4},{4,5},{5,6},{6,7},{7,8},{8,9},{9,10},{10,1... | collective-permute-start | bytes 110600 | tf_op jit(solution)/shard_map/ppermute | solution.py:342
  96.4 8.2 %collective-permute-start.5 = (bf16[1,18,1024]{2,1,0:T(8,128)(2,1)S(1)}, bf16[1,18,1024]{2,1,0:T(8,128)(2,1)S(1)}, u32[]{:S(2)}, u32[]{:S(2)}) collective-permute-start(bf16[1,18,1024]{2,1,0:T(8,128)(2,1)S(1)} %get-tuple-element.28), channel_id=1, source_target_pairs={{0,17},{1,18},{2,19},{3,20},{4,21},{5,22},{6,23},{7,24},{8,25},{9,... | collective-permute-start | bytes 110600 | tf_op jit(solution)/shard_map/ppermute | solution.py:342

commit v3 on v2

v3 whole, which is shorter than its diff:
```python
import functools
import math

import jax
import jax.numpy as jnp
from jax import lax
from jax.experimental import pallas as pl
from jax.experimental.pallas import tpu as pltpu
from jax.sharding import PartitionSpec as P

HEADS = 16
WIN = 12
HALF = 6
QUAD = 72
SPAN = 4 * QUAD
WIDTH = 512
HEAD = WIDTH // HEADS
GROUP = 8
MAIN = 256
REST = SPAN - MAIN
SUB = 18
WINDOWS = 4
FAR = -1e30
SCALE = math.log2(math.e) / math.sqrt(HEAD)
NT = (((1,), (1,)), ((), ()))


def dot(a, b):
    return jnp.dot(a, b, preferred_element_type=jnp.float32)


def dot_nt(a, b):
    return lax.dot_general(a, b, NT, preferred_element_type=jnp.float32)


def normalized(values, eps):
    centered = values - jnp.mean(values, axis=-1, keepdims=True)
    return centered * lax.rsqrt(jnp.mean(centered * centered, axis=-1, keepdims=True) + eps)


def softened(scores, apart, straddles):
    half = SPAN // 2
    top, bottom = scores[:half], scores[half:]
    most_top, most_bottom = jnp.max(top, axis=0, keepdims=True), jnp.max(bottom, axis=0, keepdims=True)
    if apart is None:
        most_top = most_bottom = jnp.maximum(most_top, most_bottom)
    else:
        if straddles:
            lane = lax.broadcasted_iota(jnp.int32, (1, MAIN), 1)
            from_top = jnp.where(lane < half, 0.0, apart)
            from_bottom = jnp.where(lane < half, apart, 0.0)
        else:
            from_top = jnp.full((1, MAIN), apart, jnp.float32)
            from_bottom = jnp.zeros((1, MAIN), jnp.float32)
        most = jnp.maximum(most_top + from_top, most_bottom + from_bottom)
        most_top, most_bottom = most - from_top, most - from_bottom
    top, bottom = jnp.exp2(top - most_top), jnp.exp2(bottom - most_bottom)
    total = jnp.sum(top, axis=0, keepdims=True) + jnp.sum(bottom, axis=0, keepdims=True)
    return jnp.concatenate([top.astype(jnp.bfloat16), bottom.astype(jnp.bfloat16)], axis=0), 1.0 / total


def attend_windows(fill, finish, grid_ref, wqkv_ref, wout_ref, mod_ref, scratch, copies, apart):
    hidden_ref, query_ref, keys_ref, vt_ref, scores_ref, rest_ref, att_ref = scratch
    copy_qkv, copy_out = copies
    wide = GROUP * HEAD
    lane_head = lax.broadcasted_iota(jnp.int32, (1, wide), 1) // HEAD
    same = (
        lax.broadcasted_iota(jnp.int32, (wide, wide), 0) // HEAD
        == lax.broadcasted_iota(jnp.int32, (wide, wide), 1) // HEAD
    )

    def main_rows(w):
        return pl.ds(pl.multiple_of(w * MAIN, MAIN), MAIN)

    def rest_rows(w):
        return pl.ds(pl.multiple_of(WINDOWS * MAIN + w * REST, REST), REST)

    @pl.loop(0, WINDOWS)
    def _(w):
        fill(w)
        hidden = (normalized(grid_ref[w], 1e-06) * (1.0 + mod_ref[0]) + mod_ref[1]).astype(jnp.bfloat16)
        hidden_ref[main_rows(w)] = hidden[:MAIN]
        hidden_ref[rest_rows(w)] = hidden[MAIN:]

    copy_qkv.wait()
    query_ref[...] = (dot(hidden_ref[...], wqkv_ref[:, :WIDTH]) * SCALE).astype(jnp.bfloat16)
    keys_ref[...] = dot(hidden_ref[...], wqkv_ref[:, WIDTH : 2 * WIDTH]).astype(jnp.bfloat16)
    values = dot_nt(wqkv_ref[:, 2 * WIDTH :].T, hidden_ref[...]).astype(jnp.bfloat16)
    for w in range(WINDOWS):
        vt_ref[w, :, :MAIN] = values[:, w * MAIN : (w + 1) * MAIN]
        vt_ref[w, :, MAIN:] = values[:, WINDOWS * MAIN + w * REST : WINDOWS * MAIN + (w + 1) * REST]

    @pl.loop(0, WINDOWS)
    def _(w):
        for group in range(HEADS // GROUP):
            cols = slice(group * wide, (group + 1) * wide)
            kg = jnp.concatenate([keys_ref[main_rows(w), cols], keys_ref[rest_rows(w), cols]], axis=0)
            qm, qr = query_ref[main_rows(w), cols], query_ref[rest_rows(w), cols]
            for part in range(2):
                items = range(part * GROUP // 2, (part + 1) * GROUP // 2)
                masked = jnp.concatenate([kg * (lane_head == item).astype(jnp.bfloat16) for item in items], axis=0)
                scores_ref[2 * group + part] = dot_nt(masked, qm)
            rest_ref[group] = dot_nt(kg, jnp.concatenate([qr] * GROUP, axis=0) * same.astype(jnp.bfloat16))
        rest = []
        for group in range(HEADS // GROUP):
            cols = slice(group * wide, (group + 1) * wide)
            for item in range(GROUP):
                heads = slice((group * GROUP + item) * HEAD, (group * GROUP + item + 1) * HEAD)
                start = item % (GROUP // 2) * SPAN
                scores = scores_ref[2 * group + item // (GROUP // 2), start : start + SPAN]
                weights, share = softened(scores, apart, True)
                att_ref[heads] = dot(vt_ref[w, heads], weights) * share
            weights, share = softened(rest_ref[group], apart, False)
            mixed = dot(vt_ref[w, cols], weights) * share
            own = [slice(item * HEAD, (item + 1) * HEAD) for item in range(GROUP)]
            rest.append(jnp.concatenate([mixed[part, part] for part in own], axis=0).T.astype(jnp.bfloat16))
        hidden_ref[main_rows(w)] = att_ref[...].T.astype(jnp.bfloat16)
        hidden_ref[rest_rows(w)] = jnp.concatenate(rest, axis=1)

    copy_out.wait()
    added = (1.0 + mod_ref[2]) * dot(hidden_ref[...], wout_ref[...])
    for w in range(WINDOWS):
        grid_ref[w, :MAIN] += added[w * MAIN : (w + 1) * MAIN]
        grid_ref[w, MAIN:] += added[WINDOWS * MAIN + w * REST : WINDOWS * MAIN + (w + 1) * REST]
        finish(w)


def staged(layer, wqkv_hbm, wout_hbm, wqkv_ref, wout_ref, sems):
    copies = (
        pltpu.make_async_copy(wqkv_hbm.at[layer], wqkv_ref, sems.at[0]),
        pltpu.make_async_copy(wout_hbm.at[layer], wout_ref, sems.at[1]),
    )
    for copy in copies:
        copy.start()
    return copies


def first_kernel(
    pair, tokens_hbm, wqkv_hbm, wout_hbm, mod_ref, *refs,
):
    if pair:
        first_west_hbm, *refs = refs
    moving_hbm, staying_hbm, west_hbm, corner_hbm, grid_ref, *scratch = refs
    *scratch, wqkv_ref, wout_ref, sems, tokens_ref, pieces_ref, token_sems, piece_sems, pass_sem = scratch
    ends = []
    if pair:
        ends.append(pltpu.make_async_copy(first_west_hbm, west_hbm.at[pl.ds(0, 1)], pass_sem))
        ends[-1].start()

    def brought(w):
        columns = pl.ds(w * WIN, WIN)
        return pltpu.make_async_copy(tokens_hbm.at[:, columns], tokens_ref.at[w], token_sems.at[w])

    for w in range(WINDOWS):
        brought(w).start()
    copies = staged(0, wqkv_hbm, wout_hbm, wqkv_ref, wout_ref, sems)

    def fill(w):
        brought(w).wait()
        for quad in range(4):
            for sub in range(4):
                for place in range(9):
                    i = quad // 2 * HALF + place // 3 * 2 + sub % 2
                    j = quad % 2 * HALF + place % 3 * 2 + sub // 2
                    row = quad * QUAD + sub * SUB + place * 2
                    grid_ref[w, row : row + 2] = tokens_ref[w, i, j, 2 * pair : 2 * pair + 2].astype(jnp.float32)

    def finish(w):
        for quad in range(4):
            half, block = quad // 2, 2 * w + quad % 2
            piece = pieces_ref.at[half, pl.ds(block, 1)]
            piece[0] = grid_ref[w, quad * QUAD : (quad + 1) * QUAD].astype(jnp.bfloat16)
            if block:
                target = (moving_hbm if half == pair else staying_hbm).at[pl.ds(block - 1, 1)]
            else:
                target = corner_hbm if half == pair else west_hbm.at[pl.ds(pair, 1)]
            ends.append(pltpu.make_async_copy(piece, target, piece_sems.at[half, block]))
            ends[-1].start()

    attend_windows(fill, finish, grid_ref, wqkv_ref, wout_ref, mod_ref.at[:, pl.ds(0, 1)], scratch, copies, None)
    for end in ends:
        end.wait()


def second_kernel(
    pair, apart_ref, staying_hbm, received_hbm, east_hbm, corner_hbm, wqkv_hbm, wout_hbm, mod_ref, merge_hbm, *refs,
):
    if pair:
        first_east_ref, *refs = refs
    away_ref, own_ref, back_east_ref, corner_ref, grid_ref, *scratch = refs
    if pair:
        back_east_ref[0] = first_east_ref[0]
    *scratch, wqkv_ref, wout_ref, sems, merge_ref, pieces_ref, joined_ref, merge_sem, piece_sems = scratch
    kept, got = pieces_ref.at[pair], pieces_ref.at[1 - pair]
    begins = [
        pltpu.make_async_copy(source, target, piece_sems.at[index])
        for index, (source, target) in enumerate(
            [
                (staying_hbm, kept.at[pl.ds(0, 7)]),
                (received_hbm, got.at[pl.ds(0, 7)]),
                (east_hbm.at[pl.ds(pair, 1)], kept.at[pl.ds(7, 1)]),
                (corner_hbm, got.at[pl.ds(7, 1)]),
            ]
        )
    ]
    for begin in begins:
        begin.start()
    copies = staged(1, wqkv_hbm, wout_hbm, wqkv_ref, wout_ref, sems)
    copy_merge = pltpu.make_async_copy(merge_hbm, merge_ref, merge_sem)
    copy_merge.start()
    for begin in begins:
        begin.wait()

    def fill(w):
        for quad in range(4):
            grid_ref[w, quad * QUAD : (quad + 1) * QUAD] = pieces_ref[quad // 2, 2 * w + quad % 2].astype(jnp.float32)

    def finish(w):
        for quad in range(4):
            for sub in range(4):
                start = quad * QUAD + sub * SUB
                joined_ref[w, quad * SUB : (quad + 1) * SUB, sub * WIDTH : (sub + 1) * WIDTH] = (
                    grid_ref[w, start : start + SUB].astype(jnp.bfloat16).astype(jnp.float32)
                )

    attend_windows(
        fill, finish, grid_ref, wqkv_ref, wout_ref, mod_ref.at[:, pl.ds(1, 1)], scratch, copies, apart_ref[pair]
    )
    flat = jnp.concatenate([normalized(joined_ref[w], 1e-05).astype(jnp.bfloat16) for w in range(WINDOWS)], axis=0)
    copy_merge.wait()
    merged = dot(flat, merge_ref[...])
    for block in range(8):
        w, side = divmod(block, 2)
        for half in range(2):
            start = w * QUAD + (2 * half + side) * SUB
            piece = merged[start : start + SUB].astype(jnp.bfloat16)
            if half == pair:
                target, last = own_ref, back_east_ref
            else:
                target, last = away_ref, corner_ref
            if block < 7:
                target[block] = piece
            else:
                last[last.shape[0] - 1] = piece


def last_kernel(*refs):
    count = len(refs) // 2 - 2
    sources, out_hbm, held, (out_ref, sems, out_sems) = refs[:count], refs[count], refs[count + 1 : -3], refs[-3:]
    copies = [pltpu.make_async_copy(*pair, sems.at[index]) for index, pair in enumerate(zip(sources, held))]
    for copy in copies:
        copy.start()
    for copy in copies:
        copy.wait()
    ends = []
    for half in range(2):
        for pair in range(2):
            own, back, corner = held[3 * pair : 3 * pair + 3]
            for block in range(8):
                if half != pair:
                    ref, index = (own, block - 1) if block else (held[-1], pair)
                else:
                    ref, index = (back, block - 1) if block else (corner, 0)
                for place in range(9):
                    i, j = half * 3 + place // 3, block * 3 + place % 3
                    out_ref[i, j, 2 * pair : 2 * pair + 2] = ref[index, 2 * place : 2 * place + 2]
        rows = pl.ds(half * 3, 3)
        ends.append(pltpu.make_async_copy(out_ref.at[rows], out_hbm.at[rows], out_sems.at[half]))
        ends[-1].start()
    for end in ends:
        end.wait()


def whole(*shape):
    return pl.BlockSpec(shape, lambda: (0,) * len(shape))


def struct(*shape):
    return jax.ShapeDtypeStruct(shape, jnp.bfloat16)


LIMIT = 64 * 1024 * 1024 - 64 * 1024
HBM = pl.BlockSpec(memory_space=pltpu.HBM)
LAYER_SCRATCH = [
    pltpu.VMEM((WINDOWS, SPAN, WIDTH), jnp.float32),
    pltpu.VMEM((WINDOWS * SPAN, WIDTH), jnp.bfloat16),
    pltpu.VMEM((WINDOWS * SPAN, WIDTH), jnp.bfloat16),
    pltpu.VMEM((WINDOWS * SPAN, WIDTH), jnp.bfloat16),
    pltpu.VMEM((WINDOWS, WIDTH, SPAN), jnp.bfloat16),
    pltpu.VMEM((4, HEADS // 4 * SPAN, MAIN), jnp.float32),
    pltpu.VMEM((HEADS // GROUP, SPAN, MAIN), jnp.float32),
    pltpu.VMEM((WIDTH, MAIN), jnp.float32),
    pltpu.VMEM((WIDTH, 3 * WIDTH), jnp.bfloat16),
    pltpu.VMEM((WIDTH, WIDTH), jnp.bfloat16),
    pltpu.SemaphoreType.DMA((2,)),
]
LAYER_SPECS = [HBM, HBM, whole(3, 2, WIDTH)]
LAYER_FLOPS = 2 * 4 * SPAN * (6 * WIDTH * WIDTH + 5 * 8 * SPAN * WIDTH)


def first_layer(pair, tokens, layers, passed):
    counts = (7, 7, 1 + len(passed), 1)
    return pl.pallas_call(
        functools.partial(first_kernel, pair),
        in_specs=[HBM] + LAYER_SPECS + [HBM] * len(passed),
        out_specs=[HBM] * 4,
        out_shape=[struct(n, QUAD, WIDTH) for n in counts],
        scratch_shapes=LAYER_SCRATCH
        + [
            pltpu.VMEM((WINDOWS, WIN, WIN, 4, WIDTH), jnp.bfloat16),
            pltpu.VMEM((2, 8, QUAD, WIDTH), jnp.bfloat16),
            pltpu.SemaphoreType.DMA((WINDOWS,)),
            pltpu.SemaphoreType.DMA((2, 8)),
            pltpu.SemaphoreType.DMA(()),
        ],
        compiler_params=pltpu.CompilerParams(vmem_limit_bytes=LIMIT),
        cost_estimate=pl.CostEstimate(flops=LAYER_FLOPS, bytes_accessed=5 << 20, transcendentals=16 * 4 * SPAN * SPAN),
        name=f"layer0_pair{pair}",
    )(tokens, *layers, *passed)


def second_layer(pair, apart, pieces, layers, w_merge, passed):
    counts = (7, 7, 1 + len(passed), 1)
    return pl.pallas_call(
        functools.partial(second_kernel, pair),
        in_specs=[pl.BlockSpec(memory_space=pltpu.SMEM)] + [HBM] * 4 + LAYER_SPECS + [HBM] + [whole(*p.shape) for p in passed],
        out_specs=[whole(n, SUB, 2 * WIDTH) for n in counts],
        out_shape=[struct(n, SUB, 2 * WIDTH) for n in counts],
        scratch_shapes=LAYER_SCRATCH
        + [
            pltpu.VMEM((4 * WIDTH, 2 * WIDTH), jnp.bfloat16),
            pltpu.VMEM((2, 8, QUAD, WIDTH), jnp.bfloat16),
            pltpu.VMEM((4, QUAD, 4 * WIDTH), jnp.float32),
            pltpu.SemaphoreType.DMA(()),
            pltpu.SemaphoreType.DMA((4,)),
        ],
        compiler_params=pltpu.CompilerParams(vmem_limit_bytes=LIMIT),
        cost_estimate=pl.CostEstimate(
            flops=LAYER_FLOPS + 2 * SPAN * 8 * WIDTH * WIDTH, bytes_accessed=8 << 20, transcendentals=16 * 4 * SPAN * SPAN
        ),
        name=f"layer1_pair{pair}",
    )(apart, *pieces, *layers, w_merge, *passed)


def moved(value, down, east):
    lats, lons = lax.axis_size("lat"), lax.axis_size("lon")
    pairs = [
        (lat * lons + lon, (lat + down) % lats * lons + (lon + east) % lons) for lat in range(lats) for lon in range(lons)
    ]
    return lax.ppermute(value, ("lat", "lon"), pairs)


def body(tokens, w_qkv, w_out, modulation, w_merge):
    layers = (w_qkv, w_out, jnp.swapaxes(modulation, 0, 1))
    lat, last = lax.axis_index("lat"), lax.axis_size("lat") - 1
    apart = jnp.where(jnp.stack([lat == last, lat == 0]), FAR, 0.0).astype(jnp.float32)
    firsts, passed = [], []
    for pair in range(2):
        firsts.append(first_layer(pair, tokens, layers, passed))
        passed = firsts[-1][2:3]
    beside = moved(passed[0], 0, -1)
    placed, passed = [], []
    for pair, (moving, staying, _, corner) in enumerate(firsts):
        way = 2 * pair - 1
        pieces = (staying, moved(moving, way, 0), beside, moved(corner, way, -1))
        away, own, east, corner = second_layer(pair, apart, pieces, layers, w_merge, passed)
        placed += [own, moved(away, -way, 0), moved(corner, -way, 1)]
        passed = [east]
    placed.append(moved(east, 0, 1))
    rows, cols = tokens.shape[0] // 2, tokens.shape[1] // 2
    return pl.pallas_call(
        last_kernel,
        in_specs=[HBM] * len(placed),
        out_specs=HBM,
        out_shape=struct(rows, cols, 4, 2 * WIDTH),
        scratch_shapes=[pltpu.VMEM(p.shape, p.dtype) for p in placed]
        + [
            pltpu.VMEM((rows, cols, 4, 2 * WIDTH), jnp.bfloat16),
            pltpu.SemaphoreType.DMA((len(placed),)),
            pltpu.SemaphoreType.DMA((2,)),
        ],
        compiler_params=pltpu.CompilerParams(vmem_limit_bytes=LIMIT),
        name="placing",
    )(*placed)


def solution(mesh):
    in_specs = (P("lat", "lon", None, None), P(), P(), P(), P())
    out_specs = P("lat", "lon", None, None)
    return jax.shard_map(body, mesh=mesh, in_specs=in_specs, out_specs=out_specs, check_vma=False)
```

time: 107 us -> 99.2 us (0.927)
  local copies, waits for them, and re-layouts: 12.3 us -> 0 us
  waiting for transfers between devices: 8.21 us -> 2.83 us
  Pallas kernels: 62.7 us -> 67.8 us
  starting transfers between devices: 22.9 us -> 26 us
    unnamed x25 -> x0, local copies, waits for them, and re-layouts: 12.3 us -> none
    ppermute x12 -> x10, waiting for transfers between devices: 8.21 us -> 2.83 us  [moved(): return lax.ppermute(value, ('lat', 'lon'), pairs)]
    ppermute x12 -> x10, starting transfers between devices: 22.9 us -> 26 us  [moved(): return lax.ppermute(value, ('lat', 'lon'), pairs)]
    pallas_call x2, Pallas kernels: 28.7 us -> 31.1 us  [first_layer(): pl.pallas_call(functools.partial(first_kernel, pair), in_specs=[HBM] + LA...]
    pallas_call x2, Pallas kernels: 32.3 us -> 33.8 us  [second_layer(): pl.pallas_call(functools.partial(second_kernel, pair), in_specs=[pl.Block...]
    pallas_call x1, Pallas kernels: 1.7 us -> 2.92 us  [body(): pl.pallas_call(last_kernel, in_specs=[HBM] * len(placed), out_specs=HBM,...]
  transfers between devices with their start and end apart: 12 -> 10, of which waited for: 3 -> 3; matrix products, arithmetic and copies ran while one was open for 0% -> 1% of each run, Pallas kernels for 44% -> 51%
where the time goes in v3:
time: 99.2 us; the launch traced here: 97.5 us
  Pallas kernels  67.8 us (68%)
  starting transfers between devices  26 us (26%)
  waiting for transfers between devices  2.83 us (3%)
    pallas_call x2, Pallas kernels, second_layer(): pl.pallas_call(functools.partial(second_kernel, pair), in_specs=[pl.Block...  33.8 us
    pallas_call x2, Pallas kernels, first_layer(): pl.pallas_call(functools.partial(first_kernel, pair), in_specs=[HBM] + LA...  31.1 us
    ppermute x10, starting transfers between devices, moved(): return lax.ppermute(value, ('lat', 'lon'), pairs)  26 us
    pallas_call x1, Pallas kernels, body(): pl.pallas_call(last_kernel, in_specs=[HBM] * len(placed), out_specs=HBM,...  2.92 us
    ppermute x10, waiting for transfers between devices, moved(): return lax.ppermute(value, ('lat', 'lon'), pairs)  2.83 us
  transfers between devices with their start and end apart: 10, of which 3 were waited for; matrix products, arithmetic and copies ran while one was open for 1% of the time, Pallas kernels for 51%

profile of v3, /device:TPU:1, one launch (start us, length us, event | category | flops | bytes accessed | tf_op | source)
XLA Modules:
  0.0 97.5 jit_solution(265094956742607141)
XLA Ops:
  0.0 15.5 %layer0_pair0.1 = (bf16[7,72,512]{2,1,0:T(8,128)(2,1)}, bf16[7,72,512]{2,1,0:T(8,128)(2,1)}, bf16[1,72,512]{2,1,0:T(8,128)(2,1)}, bf16[1,72,512]{2,1,0:T(8,128)(2,1)}) custom-call(bf16[12,48,4,512]{3,2,1,0:T(4,128)(2,1)} %tokens_hbm.3, bf16[2,512,1536]{2,1,0:T(8,128)(2,1)} %wqkv_hbm.7, bf16[2,512,512]{2,1,0:T(8,128)(2,1)} %wout_hbm.7, f32[3,2,512]{2,1,0:T(2,128)} %bitcast.3), custom_call_target="tpu_custom_call" | custom-call | flops 17213423616 | bytes 5242880 | tf_op jit(solution)/shard_map/layer0_pair0/pallas_call | solution.py:303
  15.5 9.1 %collective-permute-start = (bf16[7,72,512]{2,1,0:T(8,128)(2,1)}, bf16[7,72,512]{2,1,0:T(8,128)(2,1)}, u32[]{:S(2)}, u32[]{:S(2)}) collective-permute-start(bf16[7,72,512]{2,1,0:T(8,128)(2,1)} %get-tuple-element.22), channel_id=1, source_target_pairs={{0,240},{1,241},{2,242},{3,243},{4,244},{5,245},{6,246},{7,247},{8... | collective-permute-start | bytes 1548296 | tf_op jit(solution)/shard_map/ppermute | solution.py:350
  24.7 15.6 %layer0_pair1.1 = (bf16[7,72,512]{2,1,0:T(8,128)(2,1)}, bf16[7,72,512]{2,1,0:T(8,128)(2,1)}, bf16[2,72,512]{2,1,0:T(8,128)(2,1)}, bf16[1,72,512]{2,1,0:T(8,128)(2,1)}) custom-call(bf16[12,48,4,512]{3,2,1,0:T(4,128)(2,1)} %tokens_hbm.3, bf16[2,512,1536]{2,1,0:T(8,128)(2,1)} %wqkv_hbm.7, bf16[2,512,512]{2,1,0:T(8,128)(2,1)} %wout_hbm.7, f32[3,2,512]{2,1,0:T(2,128)} %bitcast.4, ...), custom_call_target="tpu_custom_call" | custom-call | flops 17213423616 | bytes 5242880 | tf_op jit(solution)/shard_map/layer0_pair1/pallas_call | solution.py:303
  40.2 1.0 %collective-permute-start.1 = (bf16[2,72,512]{2,1,0:T(8,128)(2,1)}, bf16[2,72,512]{2,1,0:T(8,128)(2,1)}, u32[]{:S(2)}, u32[]{:S(2)}) collective-permute-start(bf16[2,72,512]{2,1,0:T(8,128)(2,1)} %get-tuple-element.24), channel_id=1, source_target_pairs={{0,15},{1,0},{2,1},{3,2},{4,3},{5,4},{6,5},{7,6},{8,7},{9,8},{10,9... | collective-permute-start | bytes 442376 | tf_op jit(solution)/shard_map/ppermute | solution.py:350
  41.3 3.2 %collective-permute-start.2 = (bf16[1,72,512]{2,1,0:T(8,128)(2,1)}, bf16[1,72,512]{2,1,0:T(8,128)(2,1)}, u32[]{:S(2)}, u32[]{:S(2)}) collective-permute-start(bf16[1,72,512]{2,1,0:T(8,128)(2,1)} %get-tuple-element.25), channel_id=1, source_target_pairs={{0,255},{1,240},{2,241},{3,242},{4,243},{5,244},{6,245},{7,246},{8... | collective-permute-start | bytes 221192 | tf_op jit(solution)/shard_map/ppermute | solution.py:350
  44.5 0.8 collective-permute-start.6
  45.3 0.0 collective-permute-start.5
  45.3 0.7 add_select_fusion.apart_ref
  46.0 0.9 collective-permute-done.2.corner_hbm
  46.8 0.0 collective-permute-done.1.east_hbm
  46.8 0.0 collective-permute-done.received_hbm
  46.9 16.8 %layer1_pair0.1 = (bf16[7,18,1024]{2,1,0:T(8,128)(2,1)}, bf16[7,18,1024]{2,1,0:T(8,128)(2,1)}, bf16[1,18,1024]{2,1,0:T(8,128)(2,1)}, bf16[1,18,1024]{2,1,0:T(8,128)(2,1)}) custom-call(f32[2]{0:T(128)} %add_select_fusion.apart_ref, bf16[7,72,512]{2,1,0:T(8,128)(2,1)} %get-tuple-element.21.staying_hbm, bf16[7,72,512]{2,1,0:T(8,128)(2,1)} %collective-permute-done.received_hbm, ...), custom_call_target="tpu_custom_call" | custom-call | flops 18421383168 | bytes 8388608 | tf_op jit(solution)/shard_map/layer1_pair0/pallas_call | solution.py:324
  63.7 0.3 collective-permute-start.3
  64.0 0.0 collective-permute-done.6.corner_hbm
  64.0 0.0 collective-permute-done.5.received_hbm
  64.0 17.0 %layer1_pair1.1 = (bf16[7,18,1024]{2,1,0:T(8,128)(2,1)}, bf16[7,18,1024]{2,1,0:T(8,128)(2,1)}, bf16[2,18,1024]{2,1,0:T(8,128)(2,1)}, bf16[1,18,1024]{2,1,0:T(8,128)(2,1)}) custom-call(f32[2]{0:T(128)} %add_select_fusion.apart_ref, bf16[7,72,512]{2,1,0:T(8,128)(2,1)} %get-tuple-element.29.staying_hbm, ...), custom_call_target="tpu_custom_call" | custom-call | flops 18421383168 | bytes 8388608 | tf_op jit(solution)/shard_map/layer1_pair1/pallas_call | solution.py:324
  81.0 5.1 %collective-permute-start.7 = (bf16[7,18,1024]{2,1,0:T(8,128)(2,1)}, bf16[7,18,1024]{2,1,0:T(8,128)(2,1)}, u32[]{:S(2)}, u32[]{:S(2)}) collective-permute-start(bf16[7,18,1024]{2,1,0:T(8,128)(2,1)} %get-tuple-element.34), channel_id=1, source_target_pairs={{0,240},{1,241},{2,242},{3,243},{4,244},{5,245},{6,246},{7,247},{8... | collective-permute-start | bytes 774152 | tf_op jit(solution)/shard_map/ppermute | solution.py:350
  86.1 0.5 collective-permute-start.9
  86.7 0.0 collective-permute-start.4
  86.7 5.8 %collective-permute-start.8 = (bf16[1,18,1024]{2,1,0:T(8,128)(2,1)}, bf16[1,18,1024]{2,1,0:T(8,128)(2,1)}, u32[]{:S(2)}, u32[]{:S(2)}) collective-permute-start(bf16[1,18,1024]{2,1,0:T(8,128)(2,1)} %get-tuple-element.35), channel_id=1, source_target_pairs={{0,241},{1,242},{2,243},{3,244},{4,245},{5,246},{6,247},{7,248},{8... | collective-permute-start | bytes 110600 | tf_op jit(solution)/shard_map/ppermute | solution.py:350
  92.5 1.6 %collective-permute-done.4.refs_2_ = bf16[1,18,1024]{2,1,0:T(8,128)(2,1)} collective-permute-done((bf16[1,18,1024]{2,1,0:T(8,128)(2,1)}, bf16[1,18,1024]{2,1,0:T(8,128)(2,1)}, u32[]{:S(2)}, u32[]{:S(2)}) %collective-permute-start.4) | collective-permute-done | bytes 36896 | tf_op jit(solution)/shard_map/ppermute | solution.py:350
  94.1 0.3 collective-permute-done.8.refs_5_
  94.4 0.0 collective-permute-done.9.refs_6_
  94.4 0.0 collective-permute-done.3.refs_1_
  94.4 0.0 collective-permute-done.7.refs_4_
  94.4 2.9 %placing.1 = bf16[6,24,4,1024]{3,2,1,0:T(4,128)(2,1)} custom-call(bf16[7,18,1024]{2,1,0:T(8,128)(2,1)} %get-tuple-element.26.refs_0_, bf16[7,18,1024]{2,1,0:T(8,128)(2,1)} %collective-permute-done.3.refs_1_, bf16[1,18,1024]{2,1,0:T(8,128)(2,1)} %collective-permute-done.4.refs_2_, bf16[7,18,1024]{2,1,0:T(8,128)(2,1)} %get-tuple-element.33.refs_3_, ...), custom_call_target="tpu_custom_call" | custom-call | tf_op jit(solution)/shard_map/placing/pallas_call | solution.py:371
Async XLA Ops:
  15.5 31.3 %collective-permute-start = (bf16[7,72,512]{2,1,0:T(8,128)(2,1)}, bf16[7,72,512]{2,1,0:T(8,128)(2,1)}, u32[]{:S(2)}, u32[]{:S(2)}) collective-permute-start(bf16[7,72,512]{2,1,0:T(8,128)(2,1)} %get-tuple-element.22), channel_id=1, source_target_pairs={{0,240},{1,241},{2,242},{3,243},{4,244},{5,245},{6,246},{7,247},{8... | collective-permute-start | bytes 1548296 | tf_op jit(solution)/shard_map/ppermute | solution.py:350
  40.2 6.6 %collective-permute-start.1 = (bf16[2,72,512]{2,1,0:T(8,128)(2,1)}, bf16[2,72,512]{2,1,0:T(8,128)(2,1)}, u32[]{:S(2)}, u32[]{:S(2)}) collective-permute-start(bf16[2,72,512]{2,1,0:T(8,128)(2,1)} %get-tuple-element.24), channel_id=1, source_target_pairs={{0,15},{1,0},{2,1},{3,2},{4,3},{5,4},{6,5},{7,6},{8,7},{9,8},{10,9... | collective-permute-start | bytes 442376 | tf_op jit(solution)/shard_map/ppermute | solution.py:350
  41.3 5.6 %collective-permute-start.2 = (bf16[1,72,512]{2,1,0:T(8,128)(2,1)}, bf16[1,72,512]{2,1,0:T(8,128)(2,1)}, u32[]{:S(2)}, u32[]{:S(2)}) collective-permute-start(bf16[1,72,512]{2,1,0:T(8,128)(2,1)} %get-tuple-element.25), channel_id=1, source_target_pairs={{0,255},{1,240},{2,241},{3,242},{4,243},{5,244},{6,245},{7,246},{8... | collective-permute-start | bytes 221192 | tf_op jit(solution)/shard_map/ppermute | solution.py:350
  44.5 19.5 %collective-permute-start.6 = (bf16[1,72,512]{2,1,0:T(8,128)(2,1)}, bf16[1,72,512]{2,1,0:T(8,128)(2,1)}, u32[]{:S(2)}, u32[]{:S(2)}) collective-permute-start(bf16[1,72,512]{2,1,0:T(8,128)(2,1)} %get-tuple-element.31), channel_id=1, source_target_pairs={{0,31},{1,16},{2,17},{3,18},{4,19},{5,20},{6,21},{7,22},{8,23},{9,... | collective-permute-start | bytes 221192 | tf_op jit(solution)/shard_map/ppermute | solution.py:350
  45.3 18.7 %collective-permute-start.5 = (bf16[7,72,512]{2,1,0:T(8,128)(2,1)}, bf16[7,72,512]{2,1,0:T(8,128)(2,1)}, u32[]{:S(2)}, u32[]{:S(2)}) collective-permute-start(bf16[7,72,512]{2,1,0:T(8,128)(2,1)} %get-tuple-element.30), channel_id=1, source_target_pairs={{0,16},{1,17},{2,18},{3,19},{4,20},{5,21},{6,22},{7,23},{8,24},{9,... | collective-permute-start | bytes 1548296 | tf_op jit(solution)/shard_map/ppermute | solution.py:350
  63.7 30.8 %collective-permute-start.3 = (bf16[7,18,1024]{2,1,0:T(8,128)(2,1)}, bf16[7,18,1024]{2,1,0:T(8,128)(2,1)}, u32[]{:S(2)}, u32[]{:S(2)}) collective-permute-start(bf16[7,18,1024]{2,1,0:T(8,128)(2,1)} %get-tuple-element.27), channel_id=1, source_target_pairs={{0,16},{1,17},{2,18},{3,19},{4,20},{5,21},{6,22},{7,23},{8,24},{9,... | collective-permute-start | bytes 774152 | tf_op jit(solution)/shard_map/ppermute | solution.py:350
  81.0 13.4 %collective-permute-start.7 = (bf16[7,18,1024]{2,1,0:T(8,128)(2,1)}, bf16[7,18,1024]{2,1,0:T(8,128)(2,1)}, u32[]{:S(2)}, u32[]{:S(2)}) collective-permute-start(bf16[7,18,1024]{2,1,0:T(8,128)(2,1)} %get-tuple-element.34), channel_id=1, source_target_pairs={{0,240},{1,241},{2,242},{3,243},{4,244},{5,245},{6,246},{7,247},{8... | collective-permute-start | bytes 774152 | tf_op jit(solution)/shard_map/ppermute | solution.py:350
  86.1 8.3 %collective-permute-start.9 = (bf16[2,18,1024]{2,1,0:T(8,128)(2,1)}, bf16[2,18,1024]{2,1,0:T(8,128)(2,1)}, u32[]{:S(2)}, u32[]{:S(2)}) collective-permute-start(bf16[2,18,1024]{2,1,0:T(8,128)(2,1)} %get-tuple-element.36), channel_id=1, source_target_pairs={{0,1},{1,2},{2,3},{3,4},{4,5},{5,6},{6,7},{7,8},{8,9},{9,10},{10,1... | collective-permute-start | bytes 221192 | tf_op jit(solution)/shard_map/ppermute | solution.py:350
  86.7 7.4 %collective-permute-start.4 = (bf16[1,18,1024]{2,1,0:T(8,128)(2,1)}, bf16[1,18,1024]{2,1,0:T(8,128)(2,1)}, u32[]{:S(2)}, u32[]{:S(2)}) collective-permute-start(bf16[1,18,1024]{2,1,0:T(8,128)(2,1)} %get-tuple-element.28), channel_id=1, source_target_pairs={{0,17},{1,18},{2,19},{3,20},{4,21},{5,22},{6,23},{7,24},{8,25},{9,... | collective-permute-start | bytes 110600 | tf_op jit(solution)/shard_map/ppermute | solution.py:350
  86.7 7.8 %collective-permute-start.8 = (bf16[1,18,1024]{2,1,0:T(8,128)(2,1)}, bf16[1,18,1024]{2,1,0:T(8,128)(2,1)}, u32[]{:S(2)}, u32[]{:S(2)}) collective-permute-start(bf16[1,18,1024]{2,1,0:T(8,128)(2,1)} %get-tuple-element.35), channel_id=1, source_target_pairs={{0,241},{1,242},{2,243},{3,244},{4,245},{5,246},{6,247},{7,248},{8... | collective-permute-start | bytes 110600 | tf_op jit(solution)/shard_map/ppermute | solution.py:350
